TPU v7x, 512 devices: a whole 4x4x16 slice. The times are simulated.
512 devices in a mesh: strip: 32 (over z, core), pt: 16 (over x, y).
Axes of the slice: x: 4, y: 4, z: 16, core: 2. Of those that a mesh axis runs over, the one named last changes fastest.
Arguments:
- spectra: float32 [600, 128, 4096], P(None, 'strip', 'pt'), may hold values from 0.01 to 1
- courant: float32 [25], replicated, may hold values from 0.05 to 0.4
- wind_speed: float32 [128, 4096], P('strip', 'pt'), may hold values from 0.5 to 2
- wind_dir: float32 [128, 4096], P('strip', 'pt'), may hold values from -3.140625 to 3.140625
- sea_mask: int32 [128, 4096], P('strip', 'pt'), may hold values 0 or 1
- ice_mask: int32 [128, 4096], P('strip', 'pt'), may hold values 0 or 1
Outputs:
- new_spectra: float32 [600, 128, 4096], P(None, 'strip', 'pt')
All inputs are finite; a program needn't handle non-finite values. No bound on the sum of `sea_mask` or of `ice_mask` on one device may be relied on, other than what follows from the above.
Results may differ from a plain program's by a relative error of at most 0.000088.
Values sent between devices are 32-bit elements; how exact they have to be, the bound alone decides.
No kernel may reach another device: no remote copies, remote signals or barrier semaphores. Data moves between devices by JAX's collectives and lax.ppermute only.
A program may use at most 64 MiB of HBM per device.

v0:
```python
import jax
import jax.numpy as jnp
from jax import lax
from jax.sharding import PartitionSpec as P

NF = 25
ND = 24
SUB = 2


def with_halo(block, sides, width):
    for axis, dim in sides:
        count = lax.axis_size(axis)
        forward = [(i, i + 1) for i in range(count - 1)]
        backward = [(target, source) for source, target in forward]
        low = lax.ppermute(
            lax.slice_in_dim(block, block.shape[dim] - width, None, axis=dim), axis, forward
        )
        high = lax.ppermute(lax.slice_in_dim(block, 0, width, axis=dim), axis, backward)
        block = jnp.concatenate([low, block, high], axis=dim)
    return block


def tables(courant):
    ratio = 1.1 ** jnp.arange(NF, dtype=jnp.float32)
    theta = 2.0 * jnp.pi * jnp.arange(ND, dtype=jnp.float32) / ND
    speed_u = (courant[:, None] * jnp.cos(theta)[None, :]).reshape(-1)
    speed_v = (courant[:, None] * jnp.sin(theta)[None, :]).reshape(-1)
    return (ratio, theta, speed_u, speed_v)


def advance(core, west, east, south, north, speed_u, speed_v, sea):
    up_pos = jnp.maximum(speed_u, 0.0)[:, None, None]
    up_neg = jnp.minimum(speed_u, 0.0)[:, None, None]
    vp_pos = jnp.maximum(speed_v, 0.0)[:, None, None]
    vp_neg = jnp.minimum(speed_v, 0.0)[:, None, None]
    fresh = (
        core
        - up_pos * (core - west)
        - up_neg * (east - core)
        - vp_pos * (core - south)
        - vp_neg * (north - core)
    )
    return fresh * sea


def source(energy, wind_speed, wind_dir, ice_mask, ratio, theta):
    rows = energy.shape[1]
    cols = energy.shape[2]
    field = energy.reshape(NF, ND, rows, cols)
    weight = ratio / (ND * jnp.sum(ratio))
    first = jnp.einsum("fdyx,f->yx", field, weight, precision=lax.Precision.HIGHEST)
    second = jnp.einsum("fdyx,f->yx", field, weight * ratio, precision=lax.Precision.HIGHEST)
    mean_ratio = second / jnp.maximum(first, 0.05)
    icef = ice_mask.astype(jnp.float32)
    align = jnp.maximum(jnp.cos(theta[:, None, None] - wind_dir[None]), 0.0)
    gain = 0.05 * wind_speed[None, None] * ratio[:, None, None, None] * align[None]
    loss = 0.02 * ratio[:, None, None, None] * mean_ratio[None, None]
    net = (1.0 - icef)[None, None] * gain - loss - 0.7 * icef[None, None]
    return (field * jnp.exp(net)).reshape(NF * ND, rows, cols)


def advance_rows(field, speed_u, speed_v, sea_core):
    core = field[:, 1:-1]
    return advance(
        core,
        jnp.roll(core, 1, axis=2),
        jnp.roll(core, -1, axis=2),
        field[:, :-2],
        field[:, 2:],
        speed_u,
        speed_v,
        sea_core[None],
    )


def on_device(spectra, courant, wind_speed, wind_dir, sea_mask, ice_mask):
    ratio, theta, speed_u, speed_v = tables(courant)
    total = spectra.shape[0]
    rows = spectra.shape[1]
    groups = lax.axis_size("pt")
    per_dev = -(-total // groups)
    padded_total = per_dev * groups
    extra = padded_total - total
    padded = jnp.concatenate(
        [spectra, jnp.zeros((extra, rows, spectra.shape[2]), jnp.float32)], axis=0
    )
    speed_u_all = jnp.concatenate([speed_u, jnp.zeros((extra,), jnp.float32)])
    speed_v_all = jnp.concatenate([speed_v, jnp.zeros((extra,), jnp.float32)])
    fields = lax.all_to_all(padded, "pt", split_axis=0, concat_axis=2, tiled=True)
    start = lax.axis_index("pt") * per_dev
    local_u = lax.dynamic_slice_in_dim(speed_u_all, start, per_dev)
    local_v = lax.dynamic_slice_in_dim(speed_v_all, start, per_dev)
    sea_whole = lax.all_gather(sea_mask, "pt", axis=1, tiled=True).astype(jnp.float32)
    for step in range(SUB):
        wide = with_halo(fields, (("strip", 1),), 1)
        fields = advance_rows(wide, local_u, local_v, sea_whole)
    energy = lax.all_to_all(fields, "pt", split_axis=2, concat_axis=0, tiled=True)[:total]
    return source(energy, wind_speed, wind_dir, ice_mask, ratio, theta)


def solution(mesh):
    in_specs = (
        P(None, "strip", "pt"),
        P(),
        P("strip", "pt"),
        P("strip", "pt"),
        P("strip", "pt"),
        P("strip", "pt"),
    )
    out_specs = P(None, "strip", "pt")
    return jax.shard_map(
        on_device, mesh=mesh, in_specs=in_specs, out_specs=out_specs, check_vma=False
    )
```

profile of v0, /device:TPU:97, one launch (start us, length us, event | category | flops | bytes accessed | tf_op | source)
XLA Modules:
  0.0 205.9 jit_solution(6769217191840463108)
XLA Ops:
  0.0 3.6 %concatenate.37 = f32[608,4,256]{2,1,0:T(4,128)} pad(f32[600,4,256]{2,1,0:T(4,128)} %param.6, f32[]{:T(128)} %constant.12.clone.1), padding=0_8x0_0x0_0 | pad | bytes 4947972 | tf_op jit(solution)/shard_map/concatenate | solution.py:85
  3.6 6.9 %all-to-all-start = ((f32[608,4,256]{2,1,0:T(4,128)}), f32[608,4,256]{2,1,0:T(4,128)S(1)}, u32[]{:S(2)}, u32[]{:S(2)}) async-start(f32[608,4,256]{2,1,0:T(4,128)} %concatenate.37), calls=%async_computation | async-start | bytes 4980736 | tf_op jit(solution)/shard_map/all_to_all | solution.py:90
  10.9 42.2 %all_gather.3 = s32[4,4096]{1,0:T(4,128)S(1)} all-gather(s32[4,256]{1,0:T(4,128)S(1)} %copy-done), channel_id=1, replica_groups=mesh['strip'=32,'pt'=16] {'pt'}, dimensions={1}, use_global_device_ids=true | all-gather | bytes 69632 | tf_op jit(solution)/shard_map/all_gather | solution.py:94
  53.0 0.1 broadcast_maximum_fusion
  53.1 2.2 %copy.31 = f32[16,38,4,256]{3,0,1,2:T(8,128)} copy(f32[16,38,4,256]{3,2,1,0:T(4,128)S(1)} %bitcast.45) | data formatting | bytes 4980736 | tf_op jit(solution)/shard_map/all_to_all | solution.py:90
  55.4 1.9 all_to_all.29
  57.3 0.1 fusion.41
  57.4 0.6 copy.12
  58.0 10.5 %collective-permute-start = (f32[38,1,4096]{2,1,0:T(1,128)S(1)}, f32[38,1,4096]{2,1,0:T(1,128)S(1)}, u32[]{:S(2)}, u32[]{:S(2)}) collective-permute-start(f32[38,1,4096]{2,1,0:T(1,128)S(1)} %copy.12), channel_id=1, source_target_pairs={{0,16},{16,32},{32,48},{48,64},{64,80},{80,96},{96,112},{112,128},... | collective-permute-start | bytes 1867784 | tf_op jit(solution)/shard_map/ppermute | solution.py:16
  68.5 0.6 copy.14
  69.2 1.9 collective-permute-start.1
  71.1 1.0 fusion.39
  72.1 0.1 fusion.40
  72.2 3.5 %collective-permute-done = f32[38,1,4096]{2,1,0:T(1,128)S(1)} collective-permute-done((f32[38,1,4096]{2,1,0:T(1,128)S(1)}, f32[38,1,4096]{2,1,0:T(1,128)S(1)}, u32[]{:S(2)}, u32[]{:S(2)}) %collective-permute-start) | collective-permute-done | bytes 622624 | tf_op jit(solution)/shard_map/ppermute | solution.py:16
  75.7 0.4 copy.13
  76.1 5.9 %collective-permute-done.1 = f32[38,1,4096]{2,1,0:T(1,128)S(1)} collective-permute-done((f32[38,1,4096]{2,1,0:T(1,128)S(1)}, f32[38,1,4096]{2,1,0:T(1,128)S(1)}, u32[]{:S(2)}, u32[]{:S(2)}) %collective-permute-start.1) | collective-permute-done | bytes 622624 | tf_op jit(solution)/shard_map/ppermute | solution.py:19
  81.9 0.4 copy.15
  82.3 2.3 %fusion.10 = f32[38,4,4096]{2,0,1:T(8,128)S(1)} fusion(f32[38,4,4096]{2,0,1:T(8,128)S(1)} %all_to_all.29, f32[38,1,4096]{2,0,1:T(8,128)S(1)} %copy.15, f32[38,1,4096]{2,0,1:T(8,128)S(1)} %copy.13, f32[38,4,4095]{2,0,1:T(8,128)S(1)} %get-tuple-element.12, f32[38,4,1]{2,0,1:T(8,128)S(1)} %get-tuple-element.14, f32[38,4,1]{2,0,1:T(8,128)S(1)} %get-tuple-element.13, ...), kind=kLoop, calls=%fused_computation.13 | loop fusion | flops 10584064 | bytes 11272800 | tf_op jit(solution)/shard_map/mul | solution.py:44
  84.6 0.1 fusion.38
  84.7 0.6 copy.16
  85.3 1.9 collective-permute-start.2
  87.3 0.6 copy.18
  87.9 2.6 %collective-permute-start.3 = (f32[38,1,4096]{2,1,0:T(1,128)S(1)}, f32[38,1,4096]{2,1,0:T(1,128)S(1)}, u32[]{:S(2)}, u32[]{:S(2)}) collective-permute-start(f32[38,1,4096]{2,1,0:T(1,128)S(1)} %copy.18), channel_id=1, source_target_pairs={{16,0},{32,16},{48,32},{64,48},{80,64},{96,80},{112,96},{128,112},... | collective-permute-start | bytes 1867784 | tf_op jit(solution)/shard_map/ppermute | solution.py:19
  90.5 0.9 fusion.36
  91.5 0.1 fusion.37
  91.6 2.9 %collective-permute-done.2 = f32[38,1,4096]{2,1,0:T(1,128)S(1)} collective-permute-done((f32[38,1,4096]{2,1,0:T(1,128)S(1)}, f32[38,1,4096]{2,1,0:T(1,128)S(1)}, u32[]{:S(2)}, u32[]{:S(2)}) %collective-permute-start.2) | collective-permute-done | bytes 622624 | tf_op jit(solution)/shard_map/ppermute | solution.py:16
  94.4 0.4 copy.17
  94.8 5.9 %collective-permute-done.3 = f32[38,1,4096]{2,1,0:T(1,128)S(1)} collective-permute-done((f32[38,1,4096]{2,1,0:T(1,128)S(1)}, f32[38,1,4096]{2,1,0:T(1,128)S(1)}, u32[]{:S(2)}, u32[]{:S(2)}) %collective-permute-start.3) | collective-permute-done | bytes 622624 | tf_op jit(solution)/shard_map/ppermute | solution.py:19
  100.7 0.4 copy.19
  101.1 2.4 %fusion.3 = f32[38,4,4096]{2,0,1:T(8,128)S(1)} fusion(f32[38,4,4096]{2,0,1:T(8,128)S(1)} %fusion.10, f32[38,1,4096]{2,0,1:T(8,128)S(1)} %copy.19, f32[38,1,4096]{2,0,1:T(8,128)S(1)} %copy.17, f32[38,4,4095]{2,0,1:T(8,128)S(1)} %get-tuple-element.6, f32[38,4,1]{2,0,1:T(8,128)S(1)} %get-tuple-element.8, f32[38,4,1]{2,0,1:T(8,128)S(1)} %get-tuple-element.7, ...), kind=kLoop, calls=%fused_computation.4 | loop fusion | flops 10584064 | bytes 11272800 | tf_op jit(solution)/shard_map/mul | solution.py:44
  103.4 6.0 %copy.20 = f32[38,4,4096]{0,1,2:T(4,128)} copy(f32[38,4,4096]{2,0,1:T(8,128)S(1)} %fusion.3) | data formatting | bytes 4980736 | tf_op jit(solution)/shard_map/mul | solution.py:44
  109.4 13.9 %reshape.69 = f32[16,1,38912]{2,1,0:T(1,128)} reshape(f32[4096,4,38]{2,1,0:T(4,128)} %bitcast.42) | data formatting | bytes 4980736
  123.4 4.1 %all-to-all-start.1 = ((f32[16,1,38912]{2,1,0:T(1,128)}), f32[16,1,38912]{2,1,0:T(1,128)S(1)}, u32[]{:S(2)}, u32[]{:S(2)}) async-start(f32[16,1,38912]{2,1,0:T(1,128)} %reshape.69), calls=%async_computation.1 | async-start | bytes 4980736 | tf_op jit(solution)/shard_map/all_to_all | solution.py:98
  127.5 0.6 fusion.31
  128.9 0.4 cosine_maximum_fusion
  129.4 1.6 broadcast_multiply_fusion
  131.0 29.8 %all-to-all-done.1 = f32[16,1,38912]{2,1,0:T(1,128)S(1)} async-done(((f32[16,1,38912]{2,1,0:T(1,128)}), f32[16,1,38912]{2,1,0:T(1,128)S(1)}, u32[]{:S(2)}, u32[]{:S(2)}) %all-to-all-start.1) | async-done | bytes 2490400 | tf_op jit(solution)/shard_map/all_to_all | solution.py:98
  160.8 0.5 broadcast.125
  161.3 8.7 %reduce = f32[16,38912]{1,0:T(8,128)} reduce(f32[16,1,38912]{2,1,0:T(1,128)S(1)} %all-to-all-done.1, f32[]{:T(128)} %broadcast.125), dimensions={1}, to_apply=%all_to_all.30.reduce_sub_computation | reduce | bytes 4980740 | tf_op jit(solution)/shard_map/all_to_all | solution.py:98
  170.1 16.3 %reshape.70 = f32[4096,4,38]{2,1,0:T(4,128)} reshape(f32[16,38912]{1,0:T(8,128)} %reduce) | data formatting | bytes 4980736
  186.4 8.2 %copy.27 = f32[38,4,16,256]{3,0,2,1:T(8,128)} copy(f32[38,4,16,256]{0,1,3,2:T(4,128)} %bitcast.43) | data formatting | bytes 4980736 | tf_op jit(solution)/shard_map/all_to_all | solution.py:98
  194.6 2.5 %all_to_all.33 = f32[608,4,256]{2,0,1:T(8,128)S(1)} reshape(f32[16,38,4,256]{3,1,0,2:T(8,128)} %bitcast.44) | data formatting | bytes 4980736 | tf_op jit(solution)/shard_map/all_to_all | solution.py:98
  197.1 1.7 slice.88
  198.7 2.0 reduce_sum.16
  200.8 0.2 fusion.26
  201.0 0.2 fusion.28
  201.3 2.2 %fusion.24 = f32[600,4,256]{2,0,1:T(8,128)S(1)} fusion(f32[25,24,4,256]{3,1,0,2:T(8,128)} %broadcast_multiply_fusion, f32[4,256]{1,0:T(4,128)S(1)} %get-tuple-element.18, f32[25,4,256]{2,0,1:T(8,128)S(1)} %broadcast_multiply_fusion.1, f32[4,256]{1,0:T(4,128)S(1)} %get-tuple-element.17, f32[608,4,256]{2,0,1:T(8,128)S(1)} %all_to_all.33), kind=kLoop, calls=%fused_computation.34 | loop fusion | flops 2457600 | bytes 7483392 | tf_op jit(solution)/shard_map/mul | solution.py:60
  203.5 2.4 %copy.23 = f32[600,4,256]{2,1,0:T(4,128)} copy(f32[600,4,256]{2,0,1:T(8,128)S(1)} %fusion.24) | data formatting | bytes 4915200 | tf_op jit(solution)/shard_map/mul | solution.py:60
  (25 shorter events, 0.6 us)
Async XLA Ops:
  3.6 7.0 %copy-start.4 = (f32[25]{0:T(128)S(1)}, f32[25]{0:T(128)}, u32[]{:S(2)}) copy-start(f32[25]{0:T(128)} %param.7) | copy-start | bytes 304
  3.6 7.3 %copy-start = (s32[4,256]{1,0:T(4,128)S(1)}, s32[4,256]{1,0:T(4,128)}, u32[]{:S(2)}) copy-start(s32[4,256]{1,0:T(4,128)} %param.10) | copy-start | bytes 12292
  3.6 49.5 %all-to-all-start = ((f32[608,4,256]{2,1,0:T(4,128)}), f32[608,4,256]{2,1,0:T(4,128)S(1)}, u32[]{:S(2)}, u32[]{:S(2)}) async-start(f32[608,4,256]{2,1,0:T(4,128)} %concatenate.37), calls=%async_computation | async-start | bytes 4980736 | tf_op jit(solution)/shard_map/all_to_all | solution.py:90
  58.0 17.6 %collective-permute-start = (f32[38,1,4096]{2,1,0:T(1,128)S(1)}, f32[38,1,4096]{2,1,0:T(1,128)S(1)}, u32[]{:S(2)}, u32[]{:S(2)}) collective-permute-start(f32[38,1,4096]{2,1,0:T(1,128)S(1)} %copy.12), channel_id=1, source_target_pairs={{0,16},{16,32},{32,48},{48,64},{64,80},{80,96},{96,112},{112,128},... | collective-permute-start | bytes 1867784 | tf_op jit(solution)/shard_map/ppermute | solution.py:16
  69.2 12.8 %collective-permute-start.1 = (f32[38,1,4096]{2,1,0:T(1,128)S(1)}, f32[38,1,4096]{2,1,0:T(1,128)S(1)}, u32[]{:S(2)}, u32[]{:S(2)}) collective-permute-start(f32[38,1,4096]{2,1,0:T(1,128)S(1)} %copy.14), channel_id=1, source_target_pairs={{16,0},{32,16},{48,32},{64,48},{80,64},{96,80},{112,96},{128,112},... | collective-permute-start | bytes 1867784 | tf_op jit(solution)/shard_map/ppermute | solution.py:19
  85.3 9.1 %collective-permute-start.2 = (f32[38,1,4096]{2,1,0:T(1,128)S(1)}, f32[38,1,4096]{2,1,0:T(1,128)S(1)}, u32[]{:S(2)}, u32[]{:S(2)}) collective-permute-start(f32[38,1,4096]{2,1,0:T(1,128)S(1)} %copy.16), channel_id=1, source_target_pairs={{0,16},{16,32},{32,48},{48,64},{64,80},{80,96},{96,112},{112,128},... | collective-permute-start | bytes 1867784 | tf_op jit(solution)/shard_map/ppermute | solution.py:16
  87.9 12.8 %collective-permute-start.3 = (f32[38,1,4096]{2,1,0:T(1,128)S(1)}, f32[38,1,4096]{2,1,0:T(1,128)S(1)}, u32[]{:S(2)}, u32[]{:S(2)}) collective-permute-start(f32[38,1,4096]{2,1,0:T(1,128)S(1)} %copy.18), channel_id=1, source_target_pairs={{16,0},{32,16},{48,32},{64,48},{80,64},{96,80},{112,96},{128,112},... | collective-permute-start | bytes 1867784 | tf_op jit(solution)/shard_map/ppermute | solution.py:19
  123.4 5.4 %copy-start.3 = (f32[4,256]{1,0:T(4,128)S(1)}, f32[4,256]{1,0:T(4,128)}, u32[]{:S(2)}) copy-start(f32[4,256]{1,0:T(4,128)} %param.8) | copy-start | bytes 12292
  123.4 5.4 %copy-start.1 = (s32[4,256]{1,0:T(4,128)S(1)}, s32[4,256]{1,0:T(4,128)}, u32[]{:S(2)}) copy-start(s32[4,256]{1,0:T(4,128)} %param.11) | copy-start | bytes 12292
  123.4 5.5 %copy-start.2 = (f32[4,256]{1,0:T(4,128)S(1)}, f32[4,256]{1,0:T(4,128)}, u32[]{:S(2)}) copy-start(f32[4,256]{1,0:T(4,128)} %param.9) | copy-start | bytes 12292
  123.4 37.4 %all-to-all-start.1 = ((f32[16,1,38912]{2,1,0:T(1,128)}), f32[16,1,38912]{2,1,0:T(1,128)S(1)}, u32[]{:S(2)}, u32[]{:S(2)}) async-start(f32[16,1,38912]{2,1,0:T(1,128)} %reshape.69), calls=%async_computation.1 | async-start | bytes 4980736 | tf_op jit(solution)/shard_map/all_to_all | solution.py:98
where the time goes:
time: 207 us; the launch traced here: 206 us
  local copies, waits for them, and re-layouts  65.8 us (32%)
  waiting for transfers between devices  48 us (23%)
  blocking collectives  42.2 us (20%)
  starting transfers between devices  27.9 us (13%)
  other arithmetic  20.7 us (10%)
    all_gather x1, blocking collectives, on_device(): lax.all_gather(sea_mask, 'pt', axis=1, tiled=True).astype(jnp.float32)  42.2 us
    unnamed x12, local copies, waits for them, and re-layouts  30.3 us
    all_to_all x1, waiting for transfers between devices, on_device(): lax.all_to_all(fields, 'pt', split_axis=2, concat_axis=0, tiled=True)  29.8 us
    ppermute x2, starting transfers between devices, with_halo(): lax.ppermute(lax.slice_in_dim(block, block.shape[dim] - width, None, axis...  12.4 us
    ppermute x2, waiting for transfers between devices, with_halo(): lax.ppermute(lax.slice_in_dim(block, 0, width, axis=dim), axis, backward)  11.8 us
    all_to_all x3, local copies, waits for them, and re-layouts, on_device(): lax.all_to_all(fields, 'pt', split_axis=2, concat_axis=0, tiled=True)  11.2 us
    all_to_all x1, other arithmetic, on_device(): lax.all_to_all(fields, 'pt', split_axis=2, concat_axis=0, tiled=True)  8.73 us
    all_to_all x1, starting transfers between devices, on_device(): lax.all_to_all(padded, 'pt', split_axis=0, concat_axis=2, tiled=True)  6.89 us
  transfers between devices with their start and end apart: 6, of which 5 were waited for; matrix products, arithmetic and copies ran while one was open for 4% of the time, Pallas kernels for 0%

commit v1 on v0

v1 whole, which is shorter than its diff:
```python
import jax
import jax.numpy as jnp
import numpy as np
from jax import lax
from jax.experimental import pallas as pl
from jax.experimental.pallas import tpu as pltpu
from jax.sharding import PartitionSpec as P

NF = 25
ND = 24
NG = 3
ROWS = 4
COLS = 256
LANES = 128
PART = 5 * ND * 8
PER = 5

RATIO = np.float32(1.1) ** np.arange(NF, dtype=np.float32)
THETA = (np.float32(2.0 * np.pi) * np.arange(ND, dtype=np.float32) / np.float32(ND)).astype(np.float32)
COS = np.cos(THETA).astype(np.float32)
SIN = np.sin(THETA).astype(np.float32)
EAST = COS > 0
UP = SIN >= 0
WEIGHT = (RATIO / (np.float32(ND) * RATIO.sum(dtype=np.float32))).astype(np.float32)


def iotas():
    return (
        lax.broadcasted_iota(jnp.int32, (8, LANES), 0),
        lax.broadcasted_iota(jnp.int32, (8, LANES), 1),
    )


def by_sublane(values, sub):
    out = jnp.full((8, LANES), float(values[0]), jnp.float32)
    for j in range(1, 8):
        out = jnp.where(sub == j, float(values[j]), out)
    return out


def direction_tables(sub):
    cu = [by_sublane(np.abs(COS[8 * g : 8 * g + 8]), sub) for g in range(NG)]
    cv = [by_sublane(np.abs(SIN[8 * g : 8 * g + 8]), sub) for g in range(NG)]
    return cu, cv


def east_mask(g, sub):
    if g == 0:
        return sub < 6
    if g == 2:
        return sub >= 2
    return None


def roll(x, shift, axis=1):
    size = x.shape[axis]
    if isinstance(shift, int):
        shift = shift % size
        if shift == 0:
            return x
    return pltpu.roll(x, shift, axis)


def upwind_x(e, edge, sub, lane):
    first, last = lane == 0, lane == LANES - 1
    low, mid, high = e
    both = [jnp.where(sub < 2, high[c], low[c]) for c in (0, 1)]
    both_edge = jnp.where(sub < 2, edge[2], edge[0])

    def from_east(v, beside):
        l0, l1 = roll(v[0], -1), roll(v[1], -1)
        return jnp.where(last, l1, l0), jnp.where(last, beside, l1)

    def from_west(v, beside):
        r0, r1 = roll(v[0], 1), roll(v[1], 1)
        return jnp.where(first, beside, r0), jnp.where(first, r0, r1)

    be, me = from_east(both, both_edge), from_east(mid, edge[1])
    lw, hw = from_west(low, edge[0]), from_west(high, edge[2])
    return [
        [jnp.where(sub < 6, lw[c], be[c]) for c in (0, 1)],
        list(me),
        [jnp.where(sub < 2, be[c], hw[c]) for c in (0, 1)],
    ]


def upwind_y(rows, r, g, sub):
    low = rows[r - 1] if r > 0 else None
    high = rows[r + 1] if r < ROWS - 1 else None
    if g == 0:
        return low
    if g == 2:
        return high
    zero = jnp.zeros((8, LANES), jnp.float32)
    return jnp.where(sub < 4, zero if low is None else low, zero if high is None else high)


def comp_rows(i, g, r, c):
    return pl.ds((i * ND + g * 8) * 8 + c * ROWS + r, 8, 8)


def packed_plus(sub, lane):
    group = (lane // 8) % NG
    d = group * 8 + sub
    return (d < 6) | (d >= 18)


def spread(x, lane):
    x = jnp.where(lane < 8, x, 0.0)
    for step in (8, 16, 32, 64):
        x = x + roll(x, step)
    return x


def edges_kernel(spec_hbm, sea_hbm, x_out, spec, sea, sems):
    sub, lane = iotas()

    def fetch(block):
        part = pl.ds(pl.multiple_of(block * PART, PART), PART)
        return pltpu.make_async_copy(spec_hbm.at[part], spec.at[part], sems.at[block])

    for block in range(NF // PER):
        fetch(block).start()
    sea_copy = pltpu.make_async_copy(sea_hbm, sea, sems.at[NF // PER])
    sea_copy.start()
    here = lane // 2
    shifted = ((lane + 2) & (LANES - 1)) // 2
    plus_at = packed_plus(sub, lane)

    def freqs(block, carry):
        fetch(block).wait()
        easts = wests = jnp.zeros((8, LANES), jnp.float32)
        for t in range(PER):
            i = block * PER + t
            for g in range(NG):
                plus = east_mask(g, sub)
                for r in range(ROWS):
                    v = spec[comp_rows(i, g, r, 0), :]
                    if plus is not None:
                        v = jnp.where(plus, spec[comp_rows(i, g, r, 1), :], v)
                    place = 4 * (NG * t + g) + r
                    v = roll(v, 2 * place)
                    wests = jnp.where(here == place, v, wests)
                    if plus is not None:
                        easts = jnp.where(shifted == place, v, easts)
        x_out[block] = jnp.where(plus_at, roll(easts, 2), wests)
        return carry

    lax.fori_loop(0, NF // PER, freqs, 0)
    sea_copy.wait()
    seaf = sea[...].astype(jnp.float32)
    slot_e = jnp.zeros((8, LANES), jnp.float32)
    slot_w = jnp.zeros((8, LANES), jnp.float32)
    for r in range(ROWS):
        last = jnp.broadcast_to(roll(seaf, 1)[ROWS + r : ROWS + r + 1, 0:1], (8, LANES))
        first = jnp.broadcast_to(seaf[r : r + 1, 0:1], (8, LANES))
        here = (lane == 2 * r) | (lane == 2 * r + 1)
        slot_e = jnp.where(here, last, slot_e)
        slot_w = jnp.where(here, first, slot_w)
    x_out[PER] = spread(slot_e, lane)
    x_out[PER + 1] = spread(slot_w, lane)


def rows_kernel(spec, odd_ref, z_out, a_out):
    sub, _ = iotas()
    odd = odd_ref[0] == 1
    half = sub < 4

    def freqs(block, carry):
        for t in range(PER):
            i = block * PER + t
            load = lambda g, r, c: spec[comp_rows(i, g, r, c), :]
            ups = [load(0, 3, 0), load(0, 3, 1), load(0, 2, 0), load(0, 2, 1)]
            ups += [jnp.where(half, load(1, 3, c), roll(load(1, 2, c), 4, 0)) for c in (0, 1)]
            downs = [load(2, 0, 0), load(2, 0, 1), load(2, 1, 0), load(2, 1, 1)]
            downs += [jnp.where(half, roll(load(1, 1, c), 4, 0), load(1, 0, c)) for c in (0, 1)]
            for j in range(6):
                z_out[i * 6 + j] = jnp.where(odd, ups[j], downs[j])
                a_out[i * 6 + j] = jnp.where(odd, downs[j], ups[j])
        return carry

    lax.fori_loop(0, NF // PER, freqs, 0)


def copy_rows(src, dst):
    def some(j, carry):
        for t in range(10):
            dst[j * 10 + t] = src[j * 10 + t]
        return carry

    lax.fori_loop(0, NF * 6 // 10, some, 0)


def join_kernel(b_in, c_in, sea, even_ref, rows, out, rows_out):
    sub, lane = iotas()
    plus = packed_plus(sub, lane)
    even = even_ref[0] == 1
    for j in range(PER):
        west = jnp.where(even, c_in[j], b_in[j])
        east = jnp.where(even, b_in[j], c_in[j])
        out[j] = jnp.where(plus, west, east)
    west = jnp.where(even, c_in[PER], b_in[PER])
    east = jnp.where(even, b_in[PER + 1], c_in[PER + 1])
    out[PER] = jnp.where(plus, west, east)
    out[PER + 1] = sea[...].astype(jnp.float32)
    copy_rows(rows, rows_out)
    for j in range(PER + 2):
        rows_out[NF * 6 + j] = out[j]


def append_kernel(rows, joined, out):
    copy_rows(rows, out)
    for j in range(PER + 2):
        out[NF * 6 + j] = joined[j]


def row(x, j):
    return jnp.broadcast_to(x[j : j + 1, :], (8, LANES))


def gain_kernel(ratio_ref, wind_speed, wind_dir, ice, f_out, align):
    sub, lane = iotas()
    icef = ice[...].astype(jnp.float32)
    blow = (1.0 - icef) * 0.05 * wind_speed[...]
    cw, sw = jnp.cos(wind_dir[...]), jnp.sin(wind_dir[...])
    for g in range(NG):
        ct = by_sublane(COS[8 * g : 8 * g + 8], sub)
        st = by_sublane(SIN[8 * g : 8 * g + 8], sub)
        for rc in range(8):
            align[g * 8 + rc] = row(blow, rc) * jnp.maximum(ct * row(cw, rc) + st * row(sw, rc), 0.0)

    def freqs(block, carry):
        for t in range(PER):
            i = block * PER + t
            ratio = ratio_ref[i]
            for rc in range(8):
                cold = 0.7 * row(icef, rc)
                for g in range(NG):
                    f_out[i * 24 + g * 8 + rc] = jnp.exp(ratio * align[g * 8 + rc] - cold)
        return carry

    lax.fori_loop(0, NF // PER, freqs, 0)


def inner_kernel(spec, courant, ratio_ref, weight_ref, sea, joined, f, pf_out, mom_out, edge2):
    sub, lane = iotas()
    cu, cv = direction_tables(sub)
    seaf = sea[...].astype(jnp.float32)
    slot = lane // 8
    group = slot % NG
    rr = (lane % 8) // 2
    plus = packed_plus(sub, lane)
    up = group * 8 + sub < 12
    cup = jnp.where(group == 0, cu[0], jnp.where(group == 1, cu[1], cu[2]))
    cvp = jnp.where(group == 0, cv[0], jnp.where(group == 1, cv[1], cv[2]))
    sea_edge = joined[PER]
    for j in range(PER):
        co = jnp.zeros((8, LANES), jnp.float32)
        for t in range(PER):
            co = jnp.where(slot // NG == t, courant[j * PER + t], co)
        au, av = co * cup, co * cvp
        m = joined[j]
        mx = jnp.where(plus, roll(m, 1), roll(m, -1))
        my = jnp.where(up, jnp.where(rr >= 1, roll(m, 2), 0.0), jnp.where(rr <= 2, roll(m, -2), 0.0))
        edge2[j] = sea_edge * ((1.0 - au - av) * m + au * mx + av * my)

    def freqs(block, mom):
        mom = list(mom)
        m1 = joined[block]
        m2 = edge2[block]
        for t in range(PER):
            i = block * PER + t
            ci = courant[i]
            ratio = ratio_ref[i]
            weight = weight_ref[i]
            total = [None] * 8
            au, av = [ci * x for x in cu], [ci * x for x in cv]
            a0 = [1.0 - x - y for x, y in zip(au, av)]
            e = [[[spec[comp_rows(i, g, r, c), :] for c in (0, 1)] for r in range(ROWS)] for g in range(NG)]
            for m in (m1, m2):
                new = [[[None, None] for _ in range(ROWS)] for _ in range(NG)]
                for r in range(ROWS):
                    edge = [roll(m, -(8 * (NG * t + g) + 2 * r + 1)) for g in range(NG)]
                    xs = upwind_x([e[g][r] for g in range(NG)], edge, sub, lane)
                    for g in range(NG):
                        for c in (0, 1):
                            val = a0[g] * e[g][r][c] + au[g] * xs[g][c]
                            y = upwind_y([e[g][q][c] for q in range(ROWS)], r, g, sub)
                            if y is not None:
                                val = val + av[g] * y
                            new[g][r][c] = val * row(seaf, c * ROWS + r)
                e = new
            for g in range(NG):
                for r in range(ROWS):
                    for c in (0, 1):
                        rc = c * ROWS + r
                        at = i * 24 + g * 8 + rc
                        total[rc] = e[g][r][c] if total[rc] is None else total[rc] + e[g][r][c]
                        pf_out[at] = e[g][r][c] * f[at]
            for rc in range(8):
                wt = weight * total[rc]
                mom[rc] = mom[rc] + wt
                mom[8 + rc] = mom[8 + rc] + wt * ratio
        return tuple(mom)

    mom = lax.fori_loop(0, NF // PER, freqs, (jnp.zeros((8, LANES), jnp.float32),) * 16)
    for j in range(16):
        mom_out[j] = mom[j]


def outer_kernel(courant, ratio_ref, weight_ref, odd_ref, pf, f, mom, z_in, a_in, joined, out_hbm, fixed, growth, out, sems):
    sub, lane = iotas()
    cu, cv = direction_tables(sub)
    odd = odd_ref[0] == 1
    half = sub < 4
    tail = NF * 6
    zsea = jnp.where(odd, a_in[tail + PER + 1], z_in[tail + PER + 1])
    hsea = jnp.where(odd, z_in[tail + PER + 1], a_in[tail + PER + 1])
    sea = joined[PER + 1]
    sea_edge = joined[PER]
    sides = []
    for first, second, beside, at in ((0, 1, zsea, 3), (3, 2, hsea, 0)):
        edge = [roll(sea_edge, -(8 * g + 2 * first + 1)) for g in range(NG)]
        s0 = [row(sea, c * ROWS + first) for c in (0, 1)]
        s1 = [row(sea, c * ROWS + second) for c in (0, 1)]
        sm = [row(beside, c * ROWS + at) for c in (0, 1)]
        sw = upwind_x([s0] * NG, edge, sub, lane)
        sides.append([[(s0[c] * (s0[c] + sm[c]), s0[c] * (sw[g][c] + sm[c]), s0[c] * sm[c], s1[c] * s0[c]) for c in (0, 1)] for g in range(NG)])
    mixed = [tuple(jnp.where(half, x, y) for x, y in zip(sides[0][1][c], sides[1][1][c])) for c in (0, 1)]
    masks = [sides[0][0], mixed, sides[1][2]]

    def fix(block, moms):
        moms = list(moms)
        below = roll(jnp.where(odd, a_in[tail + block], z_in[tail + block]), -6)
        above = jnp.where(odd, z_in[tail + block], a_in[tail + block])
        corner = [below, jnp.where(half, below, above), above]
        for t in range(PER):
            i = block * PER + t
            ci = courant[i]
            ratio = ratio_ref[i]
            weight = weight_ref[i]
            zs = [z_in[i * 6 + j] for j in range(6)]
            as_ = [a_in[i * 6 + j] for j in range(6)]
            us = [jnp.where(odd, x, y) for x, y in zip(as_, zs)]
            ds = [jnp.where(odd, y, x) for x, y in zip(as_, zs)]
            total = {}
            h1 = [us[0:2], [jnp.where(half, us[4 + c], ds[4 + c]) for c in (0, 1)], ds[0:2]]
            h2 = [us[2:4], [roll(jnp.where(half, ds[4 + c], us[4 + c]), 4, 0) for c in (0, 1)], ds[2:4]]
            hw = upwind_x(h1, [roll(corner[g], -(8 * (NG * t + g) + 1)) for g in range(NG)], sub, lane)
            for g in range(NG):
                au, av = ci * cu[g], ci * cv[g]
                a0 = 1.0 - au - av
                k1, k2, k3 = a0 * av, au * av, av * av
                for c in (0, 1):
                    t1, t2, t3, t4 = masks[g][c]
                    first = k1 * h1[g][c] * t1 + k2 * hw[g][c] * t2 + k3 * h2[g][c] * t3
                    second = k3 * h1[g][c] * t4
                    if g == 1:
                        adds = [(0, jnp.where(half, first, 0.0)), (1, jnp.where(half, second, 0.0)), (3, jnp.where(half, 0.0, first)), (2, jnp.where(half, 0.0, second))]
                    elif g == 0:
                        adds = [(0, first), (1, second)]
                    else:
                        adds = [(3, first), (2, second)]
                    for r, add in adds:
                        rc = c * ROWS + r
                        total[rc] = add if rc not in total else total[rc] + add
                        at = i * 24 + g * 8 + rc
                        fixed[at] = pf[at] + add * f[at]
            for rc in range(8):
                wt = weight * total[rc]
                moms[rc] = moms[rc] + wt
                moms[8 + rc] = moms[8 + rc] + wt * ratio
        return tuple(moms)

    moms = lax.fori_loop(0, NF // PER, fix, tuple(mom[j] for j in range(16)))

    m0 = jnp.zeros((8, LANES), jnp.float32)
    m1 = jnp.zeros((8, LANES), jnp.float32)
    for rc in range(8):
        m0 = jnp.where(sub == rc, jnp.sum(moms[rc], axis=0, keepdims=True), m0)
        m1 = jnp.where(sub == rc, jnp.sum(moms[8 + rc], axis=0, keepdims=True), m1)
    loss = 0.02 * (m1 / jnp.maximum(m0, 0.05))
    for i in range(NF):
        growth[i] = jnp.exp(-float(RATIO[i]) * loss)

    def send(block):
        part = pl.ds(pl.multiple_of(block * PART, PART), PART)
        return pltpu.make_async_copy(out.at[part], out_hbm.at[part], sems.at[block])

    def grow(block, carry):
        for t in range(PER):
            i = block * PER + t
            for rc in range(8):
                factor = jnp.broadcast_to(growth[i, rc : rc + 1, :], (8, LANES))
                for g in range(NG):
                    at = i * 24 + g * 8 + rc
                    r = rc % ROWS
                    touched = g == 1 or (g == 0 and r < 2) or (g == 2 and r >= 2)
                    val = fixed[at] if touched else pf[at]
                    out[comp_rows(i, g, r, rc // ROWS), :] = val * factor
        send(block).start()
        return carry

    lax.fori_loop(0, NF // PER, grow, 0)
    for block in range(NF // PER):
        send(block).wait()


VM = pl.BlockSpec(memory_space=pltpu.VMEM)
SM = pl.BlockSpec(memory_space=pltpu.SMEM)
HBM = pl.BlockSpec(memory_space=pltpu.HBM)


def REG(n):
    return jax.ShapeDtypeStruct((n, 8, LANES), jnp.float32)


def call(kernel, outs, ins, scratch=(), vmem=24 << 20, outspecs=None, cost=1.0):
    return pl.pallas_call(
        kernel,
        out_shape=outs,
        in_specs=ins,
        out_specs=jax.tree.map(lambda _: VM, outs) if outspecs is None else outspecs,
        scratch_shapes=list(scratch),
        compiler_params=pltpu.CompilerParams(vmem_limit_bytes=vmem),
        cost_estimate=pl.CostEstimate(flops=0, bytes_accessed=int(cost * 3.6e6), transcendentals=0),
    )


def tiles(x):
    lead = x.shape[:-2]
    x = x.reshape(lead + (ROWS, 2, LANES))
    return jnp.swapaxes(x, -3, -2).reshape(lead + (8, LANES))


def untiles(x):
    lead = x.shape[:-2]
    x = jnp.swapaxes(x.reshape(lead + (2, ROWS, LANES)), -3, -2)
    return x.reshape(lead + (ROWS, COLS))


def on_device(spectra, courant, wind_speed, wind_dir, sea_mask, ice_mask):
    ns, nq = lax.axis_size("strip"), lax.axis_size("pt")
    pair_a = [(i, i ^ 1) for i in range(ns)]
    pair_z = [(i, ((i + 1) ^ 1) - 1) for i in range(1, ns - 1)]
    pair_b = [(i, i ^ 1) for i in range(nq)]
    pair_c = [(i, (((i + 1) ^ 1) - 1) % nq) for i in range(nq)]
    odd = (lax.axis_index("strip") % 2).reshape(1).astype(jnp.int32)
    even = (1 - lax.axis_index("pt") % 2).reshape(1).astype(jnp.int32)
    ratio, weight = jnp.asarray(RATIO), jnp.asarray(WEIGHT)
    spec = tiles(spectra).reshape(NF * ND * 8, LANES)
    wind_speed, wind_dir, sea, ice = (tiles(x) for x in (wind_speed, wind_dir, sea_mask, ice_mask))
    part_sems = pltpu.SemaphoreType.DMA((NF // PER + 1,))
    whole = pltpu.VMEM((NF * ND * 8, LANES), jnp.float32)
    xmsg = call(edges_kernel, REG(PER + 2), [HBM, HBM], [whole, pltpu.VMEM((8, LANES), jnp.int32), part_sems], cost=2.0, vmem=62 << 20)(spec, sea)
    cin = lax.ppermute(xmsg, "pt", pair_c)
    bin_ = lax.ppermute(xmsg, "pt", pair_b)
    zrows, arows = call(rows_kernel, (REG(NF * 6), REG(NF * 6)), [VM, SM], cost=0.7)(spec, odd)
    f = call(gain_kernel, REG(NF * 24), [SM, VM, VM, VM], [pltpu.VMEM((24, 8, LANES), jnp.float32)], cost=1.0)(
        ratio, wind_speed, wind_dir, ice
    )
    zrows, f = lax.optimization_barrier((zrows, f))
    joined, zmsg = call(join_kernel, (REG(PER + 2), REG(NF * 6 + PER + 2)), [VM, VM, VM, SM, VM], cost=0.2)(bin_, cin, sea, even, zrows)
    zin = lax.ppermute(zmsg, "strip", pair_z)
    pf, mom = call(
        inner_kernel,
        (REG(NF * 24), REG(16)),
        [VM, SM, SM, SM, VM, VM, VM],
        [pltpu.VMEM((PER, 8, LANES), jnp.float32)],
        cost=5.0,
    )(spec, courant, ratio, weight, sea, joined, f)
    arows, mom = lax.optimization_barrier((arows, mom))
    amsg = call(append_kernel, REG(NF * 6 + PER + 2), [VM, VM], cost=0.2)(arows, joined)
    ain = lax.ppermute(amsg, "strip", pair_a)
    out = call(
        outer_kernel,
        jax.ShapeDtypeStruct((NF * ND * 8, LANES), jnp.float32),
        [SM, SM, SM, SM, VM, VM, VM, VM, VM, VM],
        [pltpu.VMEM((NF * 24, 8, LANES), jnp.float32), pltpu.VMEM((NF, 8, LANES), jnp.float32), whole, part_sems],
        outspecs=HBM,
        cost=3.0,
    )(courant, ratio, weight, odd, pf, f, mom, zin, ain, joined)
    return untiles(out.reshape(NF * ND, 8, LANES))


def solution(mesh):
    in_specs = (
        P(None, "strip", "pt"),
        P(),
        P("strip", "pt"),
        P("strip", "pt"),
        P("strip", "pt"),
        P("strip", "pt"),
    )
    return jax.shard_map(
        on_device, mesh=mesh, in_specs=in_specs, out_specs=P(None, "strip", "pt"), check_vma=False
    )
```

time: 207 us -> 33.4 us (0.16)
  the two profiles are of different devices: /device:TPU:97 before, /device:TPU:225 now
where the time goes in v1:
time: 33.4 us; the launch traced here: 33.2 us
  starting transfers between devices  17.2 us (51%)
  Pallas kernels  12 us (36%)
  waiting for transfers between devices  2.05 us (6%)
  local copies, waits for them, and re-layouts  1.72 us (5%)
    ppermute x1, starting transfers between devices, on_device(): cin = lax.ppermute(xmsg, 'pt', pair_c)  6.84 us
    ppermute x1, starting transfers between devices, on_device(): zin = lax.ppermute(zmsg, 'strip', pair_z)  6.55 us
    pallas_call x1, Pallas kernels, on_device(): call(inner_kernel, (REG(NF * 24), REG(16)), [VM, SM, SM, SM, VM, VM, VM],...  4.29 us
    pallas_call x1, Pallas kernels, on_device(): call(outer_kernel, jax.ShapeDtypeStruct((NF * ND * 8, LANES), jnp.float32...  3.18 us
    pallas_call x1, Pallas kernels, on_device(): call(edges_kernel, REG(PER + 2), [HBM, HBM], [whole, pltpu.VMEM((8, LANES...  3.05 us
    ppermute x1, starting transfers between devices, on_device(): ain = lax.ppermute(amsg, 'strip', pair_a)  1.92 us
    ppermute x1, starting transfers between devices, on_device(): bin_ = lax.ppermute(xmsg, 'pt', pair_b)  1.92 us
    ppermute x1, waiting for transfers between devices, on_device(): zin = lax.ppermute(zmsg, 'strip', pair_z)  1.78 us
  transfers between devices with their start and end apart: 4, of which 2 were waited for; matrix products, arithmetic and copies ran while one was open for 0% of the time, Pallas kernels for 17%

profile of v1, /device:TPU:225, one launch (start us, length us, event | category | flops | bytes accessed | tf_op | source)
XLA Modules:
  0.0 33.2 jit_solution(12851009597938125205)
XLA Ops:
  0.0 0.0 copy-start.3
  0.0 0.0 copy-start.4
  0.0 0.0 copy-start.5
  0.0 0.0 copy-start.6
  0.0 3.1 %shard_map.82 = f32[7,8,128]{2,1,0:T(8,128)} custom-call(f32[4800,128]{1,0:T(8,128)} %bitcast.32, s32[8,128]{1,0:T(8,128)} %bitcast.35), custom_call_target="tpu_custom_call" | custom-call | bytes 7200000 | tf_op jit(solution)/shard_map/pallas_call | solution.py:455
  3.1 6.8 %collective-permute-start.1 = (f32[7,8,128]{2,1,0:T(8,128)}, f32[7,8,128]{2,1,0:T(8,128)S(1)}, u32[]{:S(2)}, u32[]{:S(2)}) collective-permute-start(f32[7,8,128]{2,1,0:T(8,128)} %shard_map.82), channel_id=1, source_target_pairs={{0,15},{1,2},{2,1},{3,4},{4,3},{5,6},{6,5},{7,8},{8,7},{9,10},{10,... | collective-permute-start | bytes 86024 | tf_op jit(solution)/shard_map/ppermute | solution.py:456
  9.9 1.9 %collective-permute-start = (f32[7,8,128]{2,1,0:T(8,128)}, f32[7,8,128]{2,1,0:T(8,128)S(1)}, u32[]{:S(2)}, u32[]{:S(2)}) collective-permute-start(f32[7,8,128]{2,1,0:T(8,128)} %shard_map.82), channel_id=1, source_target_pairs={{0,1},{1,0},{2,3},{3,2},{4,5},{5,4},{6,7},{7,6},{8,9},{9,8},{10,11... | collective-permute-start | bytes 86024 | tf_op jit(solution)/shard_map/ppermute | solution.py:457
  11.9 0.0 copy-start
  11.9 1.7 %copy-done = f32[600,4,256]{2,1,0:T(4,128)S(1)} copy-done((f32[600,4,256]{2,1,0:T(4,128)S(1)}, f32[600,4,256]{2,1,0:T(4,128)}, u32[]{:S(2)}) %copy-start) | copy-done | bytes 2457624
  13.6 0.0 copy-start.2
  13.6 0.0 copy-start.1
  13.6 0.0 copy-start.7
  13.6 0.0 copy-start.8
  13.6 0.3 shard_map.83
  13.9 0.0 copy-done.3
  13.9 0.0 copy-done.4
  13.9 0.0 copy-done.5
  13.9 0.0 copy-done.6
  13.9 1.0 %shard_map.84.f = f32[600,8,128]{2,1,0:T(8,128)S(1)} custom-call(f32[25]{0:T(128)S(1)} %copy-done.3, f32[8,128]{1,0:T(8,128)S(1)} %bitcast.38, f32[8,128]{1,0:T(8,128)S(1)} %bitcast.39, s32[8,128]{1,0:T(8,128)S(1)} %bitcast.40), custom_call_target="tpu_custom_call" | custom-call | bytes 3600000 | tf_op jit(solution)/shard_map/pallas_call | solution.py:459
  14.9 0.0 collective-permute-done.1.c_in
  14.9 0.0 collective-permute-done.b_in
  14.9 0.0 copy-done.2
  14.9 0.1 shard_map.85
  15.1 6.5 %collective-permute-start.2 = (f32[157,8,128]{2,1,0:T(8,128)S(1)}, f32[157,8,128]{2,1,0:T(8,128)S(1)}, u32[]{:S(2)}, u32[]{:S(2)}) collective-permute-start(f32[157,8,128]{2,1,0:T(8,128)S(1)} %get-tuple-element.23), channel_id=1, source_target_pairs={{16,32},{32,16},{48,64},{64,48},{80,96},{96,80},{112,128},{128,112... | collective-permute-start | bytes 1929224 | tf_op jit(solution)/shard_map/ppermute | solution.py:464
  21.6 0.0 copy-done.1
  21.6 0.0 copy-done.7
  21.6 0.0 copy-done.8
  21.6 4.3 %shard_map.86 = (f32[600,8,128]{2,1,0:T(8,128)S(1)}, f32[16,8,128]{2,1,0:T(8,128)S(1)}) custom-call(f32[4800,128]{1,0:T(8,128)S(1)} %bitcast.34, f32[25]{0:T(128)S(1)} %copy-done.7, f32[25]{0:T(128)S(1)} %copy-done.3, f32[25]{0:T(128)S(1)} %copy-done.8, s32[8,128]{1,0:T(8,128)S(1)} %bitcast.37, f32[7,8,128]{2,1,0:T(8,128)S(1)} %get-tuple-element.17.joined, ...), custom_call_target="tpu_custom_call" | custom-call | bytes 18000000 | tf_op jit(solution)/shard_map/pallas_call | solution.py:465
  25.9 0.1 shard_map.87
  26.0 1.9 %collective-permute-start.3 = (f32[157,8,128]{2,1,0:T(8,128)S(1)}, f32[157,8,128]{2,1,0:T(8,128)S(1)}, u32[]{:S(2)}, u32[]{:S(2)}) collective-permute-start(f32[157,8,128]{2,1,0:T(8,128)S(1)} %shard_map.87), channel_id=1, source_target_pairs={{0,16},{16,0},{32,48},{48,32},{64,80},{80,64},{96,112},{112,96},{1... | collective-permute-start | bytes 1929224 | tf_op jit(solution)/shard_map/ppermute | solution.py:474
  28.0 1.8 %collective-permute-done.2.z_in = f32[157,8,128]{2,1,0:T(8,128)S(1)} collective-permute-done((f32[157,8,128]{2,1,0:T(8,128)S(1)}, f32[157,8,128]{2,1,0:T(8,128)S(1)}, u32[]{:S(2)}, u32[]{:S(2)}) %collective-permute-start.2) | collective-permute-done | bytes 643104 | tf_op jit(solution)/shard_map/ppermute | solution.py:464
  29.7 0.3 collective-permute-done.3.a_in
  30.0 3.2 %shard_map.88 = f32[4800,128]{1,0:T(8,128)} custom-call(f32[25]{0:T(128)S(1)} %copy-done.7, f32[25]{0:T(128)S(1)} %copy-done.3, f32[25]{0:T(128)S(1)} %copy-done.8, s32[1]{0:T(128)} %bitcast.odd_ref, f32[600,8,128]{2,1,0:T(8,128)S(1)} %get-tuple-element.19.pf, f32[600,8,128]{2,1,0:T(8,128)S(1)} %shard_map.84.f, f32[16,8,128]{2,1,0:T(8,128)S(1)} %get-tuple-element.22.mom, ...), custom_call_target="tpu_custom_call" | custom-call | bytes 10800000 | tf_op jit(solution)/shard_map/pallas_call | solution.py:475
Async XLA Ops:
  0.0 13.9 %copy-start.3 = (f32[25]{0:T(128)S(1)}, f32[25]{0:T(128)}, u32[]{:S(2)}) copy-start(f32[25]{0:T(128)} %constant.31.clone.ratio_ref) | copy-start | bytes 304
  0.0 13.9 %copy-start.4 = (f32[4,256]{1,0:T(4,128)S(1)}, f32[4,256]{1,0:T(4,128)}, u32[]{:S(2)}) copy-start(f32[4,256]{1,0:T(4,128)} %param.10) | copy-start | bytes 12292
  0.0 13.9 %copy-start.5 = (f32[4,256]{1,0:T(4,128)S(1)}, f32[4,256]{1,0:T(4,128)}, u32[]{:S(2)}) copy-start(f32[4,256]{1,0:T(4,128)} %param.11) | copy-start | bytes 12292
  0.0 13.9 %copy-start.6 = (s32[4,256]{1,0:T(4,128)S(1)}, s32[4,256]{1,0:T(4,128)}, u32[]{:S(2)}) copy-start(s32[4,256]{1,0:T(4,128)} %param.13) | copy-start | bytes 12292
  3.1 11.8 %collective-permute-start.1 = (f32[7,8,128]{2,1,0:T(8,128)}, f32[7,8,128]{2,1,0:T(8,128)S(1)}, u32[]{:S(2)}, u32[]{:S(2)}) collective-permute-start(f32[7,8,128]{2,1,0:T(8,128)} %shard_map.82), channel_id=1, source_target_pairs={{0,15},{1,2},{2,1},{3,4},{4,3},{5,6},{6,5},{7,8},{8,7},{9,10},{10,... | collective-permute-start | bytes 86024 | tf_op jit(solution)/shard_map/ppermute | solution.py:456
  9.9 5.0 %collective-permute-start = (f32[7,8,128]{2,1,0:T(8,128)}, f32[7,8,128]{2,1,0:T(8,128)S(1)}, u32[]{:S(2)}, u32[]{:S(2)}) collective-permute-start(f32[7,8,128]{2,1,0:T(8,128)} %shard_map.82), channel_id=1, source_target_pairs={{0,1},{1,0},{2,3},{3,2},{4,5},{5,4},{6,7},{7,6},{8,9},{9,8},{10,11... | collective-permute-start | bytes 86024 | tf_op jit(solution)/shard_map/ppermute | solution.py:457
  11.9 1.7 %copy-start = (f32[600,4,256]{2,1,0:T(4,128)S(1)}, f32[600,4,256]{2,1,0:T(4,128)}, u32[]{:S(2)}) copy-start(f32[600,4,256]{2,1,0:T(4,128)} %param.8) | copy-start | bytes 7372804
  13.6 1.4 %copy-start.2 = (s32[4,256]{1,0:T(4,128)S(1)}, s32[4,256]{1,0:T(4,128)}, u32[]{:S(2)}) copy-start(s32[4,256]{1,0:T(4,128)} %param.12) | copy-start | bytes 12292
  13.6 8.0 %copy-start.1 = (f32[600,4,256]{2,1,0:T(4,128)S(1)}, f32[600,4,256]{2,1,0:T(4,128)}, u32[]{:S(2)}) copy-start(f32[600,4,256]{2,1,0:T(4,128)} %param.8) | copy-start | bytes 7372804
  13.6 8.1 %copy-start.7 = (f32[25]{0:T(128)S(1)}, f32[25]{0:T(128)}, u32[]{:S(2)}) copy-start(f32[25]{0:T(128)} %courant.3) | copy-start | bytes 304
  13.6 8.1 %copy-start.8 = (f32[25]{0:T(128)S(1)}, f32[25]{0:T(128)}, u32[]{:S(2)}) copy-start(f32[25]{0:T(128)} %constant.32.clone.weight_ref) | copy-start | bytes 304
  15.1 14.7 %collective-permute-start.2 = (f32[157,8,128]{2,1,0:T(8,128)S(1)}, f32[157,8,128]{2,1,0:T(8,128)S(1)}, u32[]{:S(2)}, u32[]{:S(2)}) collective-permute-start(f32[157,8,128]{2,1,0:T(8,128)S(1)} %get-tuple-element.23), channel_id=1, source_target_pairs={{16,32},{32,16},{48,64},{64,48},{80,96},{96,80},{112,128},{128,112... | collective-permute-start | bytes 1929224 | tf_op jit(solution)/shard_map/ppermute | solution.py:464
  26.0 4.0 %collective-permute-start.3 = (f32[157,8,128]{2,1,0:T(8,128)S(1)}, f32[157,8,128]{2,1,0:T(8,128)S(1)}, u32[]{:S(2)}, u32[]{:S(2)}) collective-permute-start(f32[157,8,128]{2,1,0:T(8,128)S(1)} %shard_map.87), channel_id=1, source_target_pairs={{0,16},{16,0},{32,48},{48,32},{64,80},{80,64},{96,112},{112,96},{1... | collective-permute-start | bytes 1929224 | tf_op jit(solution)/shard_map/ppermute | solution.py:474

commit v2 on v1

--- a/solution.py
+++ b/solution.py
@@ -13,6 +13,7 @@
 COLS = 256
 LANES = 128
 PART = 5 * ND * 8
+PAD = 1
 PER = 5
 
 RATIO = np.float32(1.1) ** np.arange(NF, dtype=np.float32)
@@ -116,20 +117,34 @@
     sub, lane = iotas()
 
     def fetch(block):
-        part = pl.ds(pl.multiple_of(block * PART, PART), PART)
+        part = pl.ds(block * PART, PART)
         return pltpu.make_async_copy(spec_hbm.at[part], spec.at[part], sems.at[block])
 
+    sea_copy = pltpu.make_async_copy(sea_hbm, sea, sems.at[NF // PER])
+    sea_copy.start()
     for block in range(NF // PER):
         fetch(block).start()
-    sea_copy = pltpu.make_async_copy(sea_hbm, sea, sems.at[NF // PER])
-    sea_copy.start()
     here = lane // 2
     shifted = ((lane + 2) & (LANES - 1)) // 2
     plus_at = packed_plus(sub, lane)
 
-    def freqs(block, carry):
+    sea_copy.wait()
+    seaf = sea[...].astype(jnp.float32)
+    slot_e = jnp.zeros((8, LANES), jnp.float32)
+    slot_w = jnp.zeros((8, LANES), jnp.float32)
+    for r in range(ROWS):
+        last = jnp.broadcast_to(roll(seaf, 1)[ROWS + r : ROWS + r + 1, 0:1], (8, LANES))
+        first = jnp.broadcast_to(seaf[r : r + 1, 0:1], (8, LANES))
+        place = lane // 2 == r
+        slot_e = jnp.where(place, last, slot_e)
+        slot_w = jnp.where(place, first, slot_w)
+    x_out[PER] = spread(slot_e, lane)
+    x_out[PER + 1] = spread(slot_w, lane)
+
+    for block in range(NF // PER):
         fetch(block).wait()
-        easts = wests = jnp.zeros((8, LANES), jnp.float32)
+        zero = jnp.zeros((8, LANES), jnp.float32)
+        easts, wests = [zero] * 3, [zero] * 3
         for t in range(PER):
             i = block * PER + t
             for g in range(NG):
@@ -140,25 +155,10 @@
                         v = jnp.where(plus, spec[comp_rows(i, g, r, 1), :], v)
                     place = 4 * (NG * t + g) + r
                     v = roll(v, 2 * place)
-                    wests = jnp.where(here == place, v, wests)
+                    wests[g] = jnp.where(here == place, v, wests[g])
                     if plus is not None:
-                        easts = jnp.where(shifted == place, v, easts)
-        x_out[block] = jnp.where(plus_at, roll(easts, 2), wests)
-        return carry
-
-    lax.fori_loop(0, NF // PER, freqs, 0)
-    sea_copy.wait()
-    seaf = sea[...].astype(jnp.float32)
-    slot_e = jnp.zeros((8, LANES), jnp.float32)
-    slot_w = jnp.zeros((8, LANES), jnp.float32)
-    for r in range(ROWS):
-        last = jnp.broadcast_to(roll(seaf, 1)[ROWS + r : ROWS + r + 1, 0:1], (8, LANES))
-        first = jnp.broadcast_to(seaf[r : r + 1, 0:1], (8, LANES))
-        here = (lane == 2 * r) | (lane == 2 * r + 1)
-        slot_e = jnp.where(here, last, slot_e)
-        slot_w = jnp.where(here, first, slot_w)
-    x_out[PER] = spread(slot_e, lane)
-    x_out[PER + 1] = spread(slot_w, lane)
+                        easts[g] = jnp.where(shifted == place, v, easts[g])
+        x_out[block] = jnp.where(plus_at, roll(easts[0] + easts[2], 2), wests[0] + wests[1] + wests[2])
 
 
 def rows_kernel(spec, odd_ref, z_out, a_out):
@@ -180,6 +180,12 @@
         return carry
 
     lax.fori_loop(0, NF // PER, freqs, 0)
+
+
+def blocks(body, carry):
+    for block in range(NF // PER):
+        carry = body(block, carry)
+    return carry
 
 
 def copy_rows(src, dst):
@@ -204,21 +210,25 @@
     out[PER] = jnp.where(plus, west, east)
     out[PER + 1] = sea[...].astype(jnp.float32)
     copy_rows(rows, rows_out)
-    for j in range(PER + 2):
+    for j in range(PER):
         rows_out[NF * 6 + j] = out[j]
+    rows_out[NF * 6 + PER] = out[PER + 1]
+    for j in range(PER + 1, PER + 1 + PAD):
+        rows_out[NF * 6 + j] = out[PER]
 
 
 def append_kernel(rows, joined, out):
     copy_rows(rows, out)
-    for j in range(PER + 2):
+    for j in range(PER):
         out[NF * 6 + j] = joined[j]
+    out[NF * 6 + PER] = joined[PER + 1]
 
 
 def row(x, j):
     return jnp.broadcast_to(x[j : j + 1, :], (8, LANES))
 
 
-def gain_kernel(ratio_ref, wind_speed, wind_dir, ice, f_out, align):
+def gain_kernel(ratio_ref, wind_speed, wind_dir, ice, e_in, f_out, fe_out, align):
     sub, lane = iotas()
     icef = ice[...].astype(jnp.float32)
     blow = (1.0 - icef) * 0.05 * wind_speed[...]
@@ -236,13 +246,18 @@
             for rc in range(8):
                 cold = 0.7 * row(icef, rc)
                 for g in range(NG):
-                    f_out[i * 24 + g * 8 + rc] = jnp.exp(ratio * align[g * 8 + rc] - cold)
+                    at = i * 24 + g * 8 + rc
+                    value = jnp.exp(ratio * align[g * 8 + rc] - cold)
+                    fe_out[at] = value * e_in[at]
+                    r = rc % ROWS
+                    if g == 1 or (g == 0) == (r < 2):
+                        f_out[at] = value
         return carry
 
     lax.fori_loop(0, NF // PER, freqs, 0)
 
 
-def inner_kernel(spec, courant, ratio_ref, weight_ref, sea, joined, f, pf_out, mom_out, edge2):
+def inner_kernel(spec, courant, sea, joined, e_out, mom_out, edge2):
     sub, lane = iotas()
     cu, cv = direction_tables(sub)
     seaf = sea[...].astype(jnp.float32)
@@ -268,15 +283,23 @@
         mom = list(mom)
         m1 = joined[block]
         m2 = edge2[block]
+        waiting = None
+
+        def put(i, e):
+            for g in range(NG):
+                for r in range(ROWS):
+                    for c in (0, 1):
+                        e_out[i * 24 + g * 8 + c * ROWS + r] = e[g][r][c]
+
         for t in range(PER):
             i = block * PER + t
             ci = courant[i]
-            ratio = ratio_ref[i]
-            weight = weight_ref[i]
-            total = [None] * 8
+            ratio, weight = float(RATIO[i]), float(WEIGHT[i])
             au, av = [ci * x for x in cu], [ci * x for x in cv]
             a0 = [1.0 - x - y for x, y in zip(au, av)]
             e = [[[spec[comp_rows(i, g, r, c), :] for c in (0, 1)] for r in range(ROWS)] for g in range(NG)]
+            if waiting is not None:
+                put(*waiting)
             for m in (m1, m2):
                 new = [[[None, None] for _ in range(ROWS)] for _ in range(NG)]
                 for r in range(ROWS):
@@ -290,95 +313,130 @@
                                 val = val + av[g] * y
                             new[g][r][c] = val * row(seaf, c * ROWS + r)
                 e = new
-            for g in range(NG):
-                for r in range(ROWS):
-                    for c in (0, 1):
-                        rc = c * ROWS + r
-                        at = i * 24 + g * 8 + rc
-                        total[rc] = e[g][r][c] if total[rc] is None else total[rc] + e[g][r][c]
-                        pf_out[at] = e[g][r][c] * f[at]
-            for rc in range(8):
-                wt = weight * total[rc]
-                mom[rc] = mom[rc] + wt
-                mom[8 + rc] = mom[8 + rc] + wt * ratio
+            for r in range(ROWS):
+                for c in (0, 1):
+                    rc = c * ROWS + r
+                    wt = weight * (e[0][r][c] + e[1][r][c] + e[2][r][c])
+                    mom[rc] = mom[rc] + wt
+                    mom[8 + rc] = mom[8 + rc] + wt * ratio
+            waiting = (i, e)
+        put(*waiting)
         return tuple(mom)
 
-    mom = lax.fori_loop(0, NF // PER, freqs, (jnp.zeros((8, LANES), jnp.float32),) * 16)
+    mom = blocks(freqs, (jnp.zeros((8, LANES), jnp.float32),) * 16)
     for j in range(16):
         mom_out[j] = mom[j]
 
 
-def outer_kernel(courant, ratio_ref, weight_ref, odd_ref, pf, f, mom, z_in, a_in, joined, out_hbm, fixed, growth, out, sems):
+def side(up, courant, f, msg, joined, fixed, moms, store):
     sub, lane = iotas()
     cu, cv = direction_tables(sub)
-    odd = odd_ref[0] == 1
-    half = sub < 4
+    mine = sub < 4 if up else sub >= 4
+    first, second, at = (0, 1, 3) if up else (3, 2, 0)
+    main = 0 if up else 2
     tail = NF * 6
-    zsea = jnp.where(odd, a_in[tail + PER + 1], z_in[tail + PER + 1])
-    hsea = jnp.where(odd, z_in[tail + PER + 1], a_in[tail + PER + 1])
-    sea = joined[PER + 1]
-    sea_edge = joined[PER]
-    sides = []
-    for first, second, beside, at in ((0, 1, zsea, 3), (3, 2, hsea, 0)):
-        edge = [roll(sea_edge, -(8 * g + 2 * first + 1)) for g in range(NG)]
-        s0 = [row(sea, c * ROWS + first) for c in (0, 1)]
-        s1 = [row(sea, c * ROWS + second) for c in (0, 1)]
-        sm = [row(beside, c * ROWS + at) for c in (0, 1)]
-        sw = upwind_x([s0] * NG, edge, sub, lane)
-        sides.append([[(s0[c] * (s0[c] + sm[c]), s0[c] * (sw[g][c] + sm[c]), s0[c] * sm[c], s1[c] * s0[c]) for c in (0, 1)] for g in range(NG)])
-    mixed = [tuple(jnp.where(half, x, y) for x, y in zip(sides[0][1][c], sides[1][1][c])) for c in (0, 1)]
-    masks = [sides[0][0], mixed, sides[1][2]]
-
-    def fix(block, moms):
-        moms = list(moms)
-        below = roll(jnp.where(odd, a_in[tail + block], z_in[tail + block]), -6)
-        above = jnp.where(odd, z_in[tail + block], a_in[tail + block])
-        corner = [below, jnp.where(half, below, above), above]
+    sea, sea_edge, beside = joined[PER + 1], joined[PER], msg[tail + PER]
+    edge = [roll(sea_edge, -(8 * g + 2 * first + 1)) for g in range(NG)]
+    s0 = [row(sea, c * ROWS + first) for c in (0, 1)]
+    s1 = [row(sea, c * ROWS + second) for c in (0, 1)]
+    sm = [row(beside, c * ROWS + at) for c in (0, 1)]
+    masks = {}
+    for g in (main, 1):
+        sw = upwind_one(s0, edge[g], g, sub, lane)
+        masks[g] = [(s0[c] * (s0[c] + sm[c]), s0[c] * (sw[c] + sm[c]), s0[c] * sm[c], s1[c] * s0[c]) for c in (0, 1)]
+    masks[1] = [tuple(jnp.where(mine, x, 0.0) for x in masks[1][c]) for c in (0, 1)]
+
+    corners = [roll(msg[tail + block], -(2 * at + 1)) for block in range(NF // PER)]
+
+    def freqs(block, carry):
+        moms = list(carry)
+        corner = corners[block]
+        waiting = []
+
+        def put():
+            for where, value in waiting.pop(0):
+                fixed[where] = value
+
         for t in range(PER):
             i = block * PER + t
             ci = courant[i]
-            ratio = ratio_ref[i]
-            weight = weight_ref[i]
-            zs = [z_in[i * 6 + j] for j in range(6)]
-            as_ = [a_in[i * 6 + j] for j in range(6)]
-            us = [jnp.where(odd, x, y) for x, y in zip(as_, zs)]
-            ds = [jnp.where(odd, y, x) for x, y in zip(as_, zs)]
-            total = {}
-            h1 = [us[0:2], [jnp.where(half, us[4 + c], ds[4 + c]) for c in (0, 1)], ds[0:2]]
-            h2 = [us[2:4], [roll(jnp.where(half, ds[4 + c], us[4 + c]), 4, 0) for c in (0, 1)], ds[2:4]]
-            hw = upwind_x(h1, [roll(corner[g], -(8 * (NG * t + g) + 1)) for g in range(NG)], sub, lane)
-            for g in range(NG):
+            ratio, weight = float(RATIO[i]), float(WEIGHT[i])
+            m = [msg[i * 6 + j] for j in range(6)]
+            fs = [[[f[i * 24 + g * 8 + c * ROWS + r] for c in (0, 1)] for r in (first, second)] for g in (main, 1)]
+            if len(waiting) == 2:
+                put()
+            total = [[None, None], [None, None]]
+            results = []
+            for slot, g in enumerate((main, 1)):
+                h1 = m[0:2] if slot == 0 else m[4:6]
+                h2 = m[2:4] if slot == 0 else [roll(v, 4, 0) for v in m[4:6]]
+                hw = upwind_one(h1, roll(corner, -8 * (NG * t + g)), g, sub, lane)
                 au, av = ci * cu[g], ci * cv[g]
                 a0 = 1.0 - au - av
                 k1, k2, k3 = a0 * av, au * av, av * av
                 for c in (0, 1):
                     t1, t2, t3, t4 = masks[g][c]
-                    first = k1 * h1[g][c] * t1 + k2 * hw[g][c] * t2 + k3 * h2[g][c] * t3
-                    second = k3 * h1[g][c] * t4
-                    if g == 1:
-                        adds = [(0, jnp.where(half, first, 0.0)), (1, jnp.where(half, second, 0.0)), (3, jnp.where(half, 0.0, first)), (2, jnp.where(half, 0.0, second))]
-                    elif g == 0:
-                        adds = [(0, first), (1, second)]
-                    else:
-                        adds = [(3, first), (2, second)]
-                    for r, add in adds:
-                        rc = c * ROWS + r
-                        total[rc] = add if rc not in total else total[rc] + add
-                        at = i * 24 + g * 8 + rc
-                        fixed[at] = pf[at] + add * f[at]
-            for rc in range(8):
-                wt = weight * total[rc]
-                moms[rc] = moms[rc] + wt
-                moms[8 + rc] = moms[8 + rc] + wt * ratio
+                    adds = (k1 * h1[c] * t1 + k2 * hw[c] * t2 + k3 * h2[c] * t3, k3 * h1[c] * t4)
+                    for n, add in enumerate(adds):
+                        total[n][c] = add if total[n][c] is None else total[n][c] + add
+                        results.append((i * 8 + slot * 4 + n * 2 + c, add * fs[slot][n][c]))
+            for n in (0, 1):
+                for c in (0, 1):
+                    wt = weight * total[n][c]
+                    j = n * 2 + c
+                    moms[j] = moms[j] + wt
+                    moms[4 + j] = moms[4 + j] + wt * ratio
+            waiting.append(results)
+        while waiting:
+            put()
         return tuple(moms)
 
-    moms = lax.fori_loop(0, NF // PER, fix, tuple(mom[j] for j in range(16)))
+    rcs = [c * ROWS + r for r in (first, second) for c in (0, 1)]
+    start = tuple(moms[rc] for rc in rcs) + tuple(moms[8 + rc] for rc in rcs)
+    done = blocks(freqs, start)
+    for rc in range(8):
+        if rc not in rcs:
+            store[rc] = moms[rc]
+            store[8 + rc] = moms[8 + rc]
+    for j, rc in enumerate(rcs):
+        store[rc] = done[j]
+        store[8 + rc] = done[4 + j]
+
+
+def upwind_one(e, edge, g, sub, lane):
+    first, last = lane == 0, lane == LANES - 1
+    l0, l1 = roll(e[0], -1), roll(e[1], -1)
+    x0, x1 = jnp.where(last, l1, l0), jnp.where(last, edge, l1)
+    plus = east_mask(g, sub)
+    if plus is None:
+        return x0, x1
+    r0, r1 = roll(e[0], 1), roll(e[1], 1)
+    w0, w1 = jnp.where(first, edge, r0), jnp.where(first, r0, r1)
+    return jnp.where(plus, w0, x0), jnp.where(plus, w1, x1)
+
+
+def near_kernel(courant, odd_ref, f, mom, a_in, joined, fixed, mom_out):
+    for up in (True, False):
+
+        @pl.when(odd_ref[0] == (1 if up else 0))
+        def _():
+            side(up, courant, f, a_in, joined, fixed, mom, mom_out)
+
+
+def outer_kernel(courant, odd_ref, pf, f, mom, near, z_in, joined, out_hbm, far, mom2, growth, out, sems):
+    sub, _ = iotas()
+    odd = odd_ref[0] == 1
+    for up in (True, False):
+
+        @pl.when(odd_ref[0] == (0 if up else 1))
+        def _():
+            side(up, courant, f, z_in, joined, far, mom, mom2)
 
     m0 = jnp.zeros((8, LANES), jnp.float32)
     m1 = jnp.zeros((8, LANES), jnp.float32)
     for rc in range(8):
-        m0 = jnp.where(sub == rc, jnp.sum(moms[rc], axis=0, keepdims=True), m0)
-        m1 = jnp.where(sub == rc, jnp.sum(moms[8 + rc], axis=0, keepdims=True), m1)
+        m0 = jnp.where(sub == rc, jnp.sum(mom2[rc], axis=0, keepdims=True), m0)
+        m1 = jnp.where(sub == rc, jnp.sum(mom2[8 + rc], axis=0, keepdims=True), m1)
     loss = 0.02 * (m1 / jnp.maximum(m0, 0.05))
     for i in range(NF):
         growth[i] = jnp.exp(-float(RATIO[i]) * loss)
@@ -390,14 +448,20 @@
     def grow(block, carry):
         for t in range(PER):
             i = block * PER + t
+            a = [near[i * 8 + j] for j in range(8)]
+            z = [far[i * 8 + j] for j in range(8)]
+            ups = [jnp.where(odd, x, y) for x, y in zip(a, z)]
+            downs = [jnp.where(odd, y, x) for x, y in zip(a, z)]
             for rc in range(8):
+                c, r = rc // ROWS, rc % ROWS
                 factor = jnp.broadcast_to(growth[i, rc : rc + 1, :], (8, LANES))
                 for g in range(NG):
-                    at = i * 24 + g * 8 + rc
-                    r = rc % ROWS
-                    touched = g == 1 or (g == 0 and r < 2) or (g == 2 and r >= 2)
-                    val = fixed[at] if touched else pf[at]
-                    out[comp_rows(i, g, r, rc // ROWS), :] = val * factor
+                    val = pf[i * 24 + g * 8 + rc]
+                    if r < 2 and g < 2:
+                        val = val + ups[(0 if g == 0 else 4) + r * 2 + c]
+                    if r >= 2 and g > 0:
+                        val = val + downs[(0 if g == 2 else 4) + (3 - r) * 2 + c]
+                    out[comp_rows(i, g, r, c), :] = val * factor
         send(block).start()
         return carry
 
@@ -447,39 +511,45 @@
     pair_c = [(i, (((i + 1) ^ 1) - 1) % nq) for i in range(nq)]
     odd = (lax.axis_index("strip") % 2).reshape(1).astype(jnp.int32)
     even = (1 - lax.axis_index("pt") % 2).reshape(1).astype(jnp.int32)
-    ratio, weight = jnp.asarray(RATIO), jnp.asarray(WEIGHT)
+    ratio = jnp.asarray(RATIO)
     spec = tiles(spectra).reshape(NF * ND * 8, LANES)
     wind_speed, wind_dir, sea, ice = (tiles(x) for x in (wind_speed, wind_dir, sea_mask, ice_mask))
     part_sems = pltpu.SemaphoreType.DMA((NF // PER + 1,))
     whole = pltpu.VMEM((NF * ND * 8, LANES), jnp.float32)
     xmsg = call(edges_kernel, REG(PER + 2), [HBM, HBM], [whole, pltpu.VMEM((8, LANES), jnp.int32), part_sems], cost=2.0, vmem=62 << 20)(spec, sea)
+    bin_ = lax.ppermute(xmsg, "pt", pair_b)
     cin = lax.ppermute(xmsg, "pt", pair_c)
-    bin_ = lax.ppermute(xmsg, "pt", pair_b)
     zrows, arows = call(rows_kernel, (REG(NF * 6), REG(NF * 6)), [VM, SM], cost=0.7)(spec, odd)
-    f = call(gain_kernel, REG(NF * 24), [SM, VM, VM, VM], [pltpu.VMEM((24, 8, LANES), jnp.float32)], cost=1.0)(
-        ratio, wind_speed, wind_dir, ice
-    )
-    zrows, f = lax.optimization_barrier((zrows, f))
-    joined, zmsg = call(join_kernel, (REG(PER + 2), REG(NF * 6 + PER + 2)), [VM, VM, VM, SM, VM], cost=0.2)(bin_, cin, sea, even, zrows)
+    joined, zmsg = call(join_kernel, (REG(PER + 2), REG(NF * 6 + PER + 1 + PAD)), [VM, VM, VM, SM, VM], cost=0.2)(bin_, cin, sea, even, zrows)
     zin = lax.ppermute(zmsg, "strip", pair_z)
-    pf, mom = call(
+    e2, mom = call(
         inner_kernel,
         (REG(NF * 24), REG(16)),
-        [VM, SM, SM, SM, VM, VM, VM],
+        [VM, SM, VM, VM],
         [pltpu.VMEM((PER, 8, LANES), jnp.float32)],
         cost=5.0,
-    )(spec, courant, ratio, weight, sea, joined, f)
-    arows, mom = lax.optimization_barrier((arows, mom))
-    amsg = call(append_kernel, REG(NF * 6 + PER + 2), [VM, VM], cost=0.2)(arows, joined)
+    )(spec, courant, sea, joined)
+    amsg = call(append_kernel, REG(NF * 6 + PER + 1), [VM, VM], cost=0.2)(arows, joined)
     ain = lax.ppermute(amsg, "strip", pair_a)
+    ratio, _ = lax.optimization_barrier((ratio, amsg))
+    f, fe = call(gain_kernel, (REG(NF * 24), REG(NF * 24)), [SM, VM, VM, VM, VM], [pltpu.VMEM((24, 8, LANES), jnp.float32)], cost=1.0)(
+        ratio, wind_speed, wind_dir, ice, e2
+    )
+    near, mom = call(near_kernel, (REG(NF * 8), REG(16)), [SM, SM, VM, VM, VM, VM], cost=0.0)(courant, odd, f, mom, ain, joined)
     out = call(
         outer_kernel,
         jax.ShapeDtypeStruct((NF * ND * 8, LANES), jnp.float32),
-        [SM, SM, SM, SM, VM, VM, VM, VM, VM, VM],
-        [pltpu.VMEM((NF * 24, 8, LANES), jnp.float32), pltpu.VMEM((NF, 8, LANES), jnp.float32), whole, part_sems],
+        [SM, SM, VM, VM, VM, VM, VM, VM],
+        [
+            pltpu.VMEM((NF * 8, 8, LANES), jnp.float32),
+            pltpu.VMEM((16, 8, LANES), jnp.float32),
+            pltpu.VMEM((NF, 8, LANES), jnp.float32),
+            whole,
+            part_sems,
+        ],
         outspecs=HBM,
         cost=3.0,
-    )(courant, ratio, weight, odd, pf, f, mom, zin, ain, joined)
+    )(courant, odd, fe, f, mom, near, zin, joined)
     return untiles(out.reshape(NF * ND, 8, LANES))
 
 

time: 33.4 us -> 32.2 us (0.964)
  waiting for transfers between devices: 2.05 us -> 1.01 us
  Pallas kernels: 12 us -> 11.6 us
    ppermute x1, waiting for transfers between devices: 1.78 us -> 0.18 us  [on_device(): zin = lax.ppermute(zmsg, 'strip', pair_z)]
    ppermute x1, waiting for transfers between devices: 0.01 us -> 0.83 us  [on_device(): bin_ = lax.ppermute(xmsg, 'pt', pair_b)]
    pallas_call x1, Pallas kernels: 3.18 us -> 2.55 us  [on_device(): call(outer_kernel, jax.ShapeDtypeStruct((NF * ND * 8, LANES), jnp.float32...]
    pallas_call x4 -> x5, Pallas kernels: 5.46 us -> 6.01 us  [the longest x1 3.81 us: on_device(): call(inner_kernel, (REG(NF * 24), REG(16)), [VM, SM, VM, VM], [pltpu.VMEM...]
    unnamed x18 -> x16, local copies, waits for them, and re-layouts: 1.72 us -> 1.73 us
  transfers between devices with their start and end apart: 4 -> 4, of which waited for: 2 -> 2; matrix products, arithmetic and copies ran while one was open for 0% -> 0% of each run, Pallas kernels for 17% -> 19%
where the time goes in v2:
time: 32.2 us; the launch traced here: 32 us
  starting transfers between devices  17.4 us (54%)
  Pallas kernels  11.6 us (36%)
  local copies, waits for them, and re-layouts  1.73 us (5%)
  waiting for transfers between devices  1.01 us (3%)
    ppermute x1, starting transfers between devices, on_device(): cin = lax.ppermute(xmsg, 'pt', pair_c)  6.84 us
    ppermute x1, starting transfers between devices, on_device(): zin = lax.ppermute(zmsg, 'strip', pair_z)  6.75 us
    pallas_call x1, Pallas kernels, on_device(): call(inner_kernel, (REG(NF * 24), REG(16)), [VM, SM, VM, VM], [pltpu.VMEM...  3.81 us
    pallas_call x1, Pallas kernels, on_device(): call(edges_kernel, REG(PER + 2), [HBM, HBM], [whole, pltpu.VMEM((8, LANES...  2.73 us
    pallas_call x1, Pallas kernels, on_device(): call(outer_kernel, jax.ShapeDtypeStruct((NF * ND * 8, LANES), jnp.float32...  2.55 us
    ppermute x1, starting transfers between devices, on_device(): ain = lax.ppermute(amsg, 'strip', pair_a)  1.92 us
    ppermute x1, starting transfers between devices, on_device(): bin_ = lax.ppermute(xmsg, 'pt', pair_b)  1.92 us
    unnamed x16, local copies, waits for them, and re-layouts  1.73 us
  transfers between devices with their start and end apart: 4, of which 2 were waited for; matrix products, arithmetic and copies ran while one was open for 0% of the time, Pallas kernels for 19%

profile of v2, /device:TPU:225, one launch (start us, length us, event | category | flops | bytes accessed | tf_op | source)
XLA Modules:
  0.0 32.0 jit_solution(6725737941287357167)
XLA Ops:
  0.0 0.0 copy-start.2
  0.0 2.7 %shard_map.74 = f32[7,8,128]{2,1,0:T(8,128)} custom-call(f32[4800,128]{1,0:T(8,128)} %bitcast.32, s32[8,128]{1,0:T(8,128)} %bitcast.35), custom_call_target="tpu_custom_call" | custom-call | bytes 7200000 | tf_op jit(solution)/shard_map/pallas_call | solution.py:519
  2.7 0.0 copy-start.3
  2.8 6.8 %collective-permute-start.1 = (f32[7,8,128]{2,1,0:T(8,128)}, f32[7,8,128]{2,1,0:T(8,128)S(1)}, u32[]{:S(2)}, u32[]{:S(2)}) collective-permute-start(f32[7,8,128]{2,1,0:T(8,128)} %shard_map.74), channel_id=1, source_target_pairs={{0,15},{1,2},{2,1},{3,4},{4,3},{5,6},{6,5},{7,8},{8,7},{9,10},{10,... | collective-permute-start | bytes 86024 | tf_op jit(solution)/shard_map/ppermute | solution.py:521
  9.6 1.9 %collective-permute-start = (f32[7,8,128]{2,1,0:T(8,128)}, f32[7,8,128]{2,1,0:T(8,128)S(1)}, u32[]{:S(2)}, u32[]{:S(2)}) collective-permute-start(f32[7,8,128]{2,1,0:T(8,128)} %shard_map.74), channel_id=1, source_target_pairs={{0,1},{1,0},{2,3},{3,2},{4,5},{5,4},{6,7},{7,6},{8,9},{9,8},{10,11... | collective-permute-start | bytes 86024 | tf_op jit(solution)/shard_map/ppermute | solution.py:520
  11.5 0.0 copy-start
  11.6 1.7 %copy-done = f32[600,4,256]{2,1,0:T(4,128)S(1)} copy-done((f32[600,4,256]{2,1,0:T(4,128)S(1)}, f32[600,4,256]{2,1,0:T(4,128)}, u32[]{:S(2)}) %copy-start) | copy-done | bytes 2457624
  13.2 0.0 copy-start.1
  13.2 0.3 shard_map.73
  13.5 0.0 copy-start.4
  13.6 0.0 copy-start.5
  13.6 0.0 copy-start.6
  13.6 0.0 copy-start.7
  13.6 0.0 collective-permute-done.1.c_in
  13.6 0.8 %collective-permute-done.b_in = f32[7,8,128]{2,1,0:T(8,128)S(1)} collective-permute-done((f32[7,8,128]{2,1,0:T(8,128)}, f32[7,8,128]{2,1,0:T(8,128)S(1)}, u32[]{:S(2)}, u32[]{:S(2)}) %collective-permute-start) | collective-permute-done | bytes 28704 | tf_op jit(solution)/shard_map/ppermute | solution.py:520
  14.4 0.0 copy-done.2
  14.4 0.1 shard_map.75
  14.5 6.7 %collective-permute-start.3 = (f32[157,8,128]{2,1,0:T(8,128)S(1)}, f32[157,8,128]{2,1,0:T(8,128)S(1)}, u32[]{:S(2)}, u32[]{:S(2)}) collective-permute-start(f32[157,8,128]{2,1,0:T(8,128)S(1)} %get-tuple-element.26), channel_id=1, source_target_pairs={{16,32},{32,16},{48,64},{64,48},{80,96},{96,80},{112,128},{128,112... | collective-permute-start | bytes 1929224 | tf_op jit(solution)/shard_map/ppermute | solution.py:524
  21.3 0.1 shard_map.76
  21.4 1.9 %collective-permute-start.2 = (f32[156,8,128]{2,1,0:T(8,128)S(1)}, f32[156,8,128]{2,1,0:T(8,128)S(1)}, u32[]{:S(2)}, u32[]{:S(2)}) collective-permute-start(f32[156,8,128]{2,1,0:T(8,128)S(1)} %shard_map.76), channel_id=1, source_target_pairs={{0,16},{16,0},{32,48},{48,32},{64,80},{80,64},{96,112},{112,96},{1... | collective-permute-start | bytes 1916936 | tf_op jit(solution)/shard_map/ppermute | solution.py:533
  23.3 0.0 copy-done.3
  23.3 0.0 copy-done.1
  23.3 3.8 %shard_map.77 = (f32[600,8,128]{2,1,0:T(8,128)S(1)}, f32[16,8,128]{2,1,0:T(8,128)S(1)}) custom-call(f32[4800,128]{1,0:T(8,128)S(1)} %bitcast.34, f32[25]{0:T(128)S(1)} %copy-done.3, s32[8,128]{1,0:T(8,128)S(1)} %bitcast.37, f32[7,8,128]{2,1,0:T(8,128)S(1)} %get-tuple-element.18.joined), custom_call_target="tpu_custom_call" | custom-call | bytes 18000000 | tf_op jit(solution)/shard_map/pallas_call | solution.py:525
  27.1 0.0 copy-done.4
  27.2 0.0 copy-done.5
  27.2 0.0 copy-done.6
  27.2 0.0 copy-done.7
  27.2 1.1 %shard_map.78 = (f32[600,8,128]{2,1,0:T(8,128)S(1)}, f32[600,8,128]{2,1,0:T(8,128)S(1)}) custom-call(f32[25]{0:T(128)S(1)} %copy-done.7, f32[8,128]{1,0:T(8,128)S(1)} %bitcast.38, f32[8,128]{1,0:T(8,128)S(1)} %bitcast.39, s32[8,128]{1,0:T(8,128)S(1)} %bitcast.40, f32[600,8,128]{2,1,0:T(8,128)S(1)} %get-tuple-element.20.e_in), custom_call_target="tpu_custom_call" | custom-call | bytes 3600000 | tf_op jit(solution)/shard_map/pallas_call | solution.py:535
  28.3 0.0 collective-permute-done.2.a_in
  28.3 0.9 %shard_map.79 = (f32[200,8,128]{2,1,0:T(8,128)S(1)}, f32[16,8,128]{2,1,0:T(8,128)S(1)}) custom-call(f32[25]{0:T(128)S(1)} %copy-done.3, s32[1]{0:T(128)} %bitcast.odd_ref, f32[600,8,128]{2,1,0:T(8,128)S(1)} %get-tuple-element.22.f, f32[16,8,128]{2,1,0:T(8,128)S(1)} %get-tuple-element.23.mom, f32[156,8,128]{2,1,0:T(8,128)S(1)} %collective-permute-done.2.a_in, ...), custom_call_target="tpu_custom_call" | custom-call | tf_op jit(solution)/shard_map/pallas_call | solution.py:538
  29.2 0.2 collective-permute-done.3.z_in
  29.4 2.5 %shard_map.80 = f32[4800,128]{1,0:T(8,128)} custom-call(f32[25]{0:T(128)S(1)} %copy-done.3, s32[1]{0:T(128)} %bitcast.odd_ref, f32[600,8,128]{2,1,0:T(8,128)S(1)} %get-tuple-element.21.pf, f32[600,8,128]{2,1,0:T(8,128)S(1)} %get-tuple-element.22.f, f32[16,8,128]{2,1,0:T(8,128)S(1)} %get-tuple-element.24.mom, f32[200,8,128]{2,1,0:T(8,128)S(1)} %get-tuple-element.25.near, ...), custom_call_target="tpu_custom_call" | custom-call | bytes 10800000 | tf_op jit(solution)/shard_map/pallas_call | solution.py:539
Async XLA Ops:
  0.0 14.4 %copy-start.2 = (s32[4,256]{1,0:T(4,128)S(1)}, s32[4,256]{1,0:T(4,128)}, u32[]{:S(2)}) copy-start(s32[4,256]{1,0:T(4,128)} %param.11) | copy-start | bytes 12292
  2.7 20.6 %copy-start.3 = (f32[25]{0:T(128)S(1)}, f32[25]{0:T(128)}, u32[]{:S(2)}) copy-start(f32[25]{0:T(128)} %courant.5) | copy-start | bytes 304
  2.8 10.8 %collective-permute-start.1 = (f32[7,8,128]{2,1,0:T(8,128)}, f32[7,8,128]{2,1,0:T(8,128)S(1)}, u32[]{:S(2)}, u32[]{:S(2)}) collective-permute-start(f32[7,8,128]{2,1,0:T(8,128)} %shard_map.74), channel_id=1, source_target_pairs={{0,15},{1,2},{2,1},{3,4},{4,3},{5,6},{6,5},{7,8},{8,7},{9,10},{10,... | collective-permute-start | bytes 86024 | tf_op jit(solution)/shard_map/ppermute | solution.py:521
  9.6 4.8 %collective-permute-start = (f32[7,8,128]{2,1,0:T(8,128)}, f32[7,8,128]{2,1,0:T(8,128)S(1)}, u32[]{:S(2)}, u32[]{:S(2)}) collective-permute-start(f32[7,8,128]{2,1,0:T(8,128)} %shard_map.74), channel_id=1, source_target_pairs={{0,1},{1,0},{2,3},{3,2},{4,5},{5,4},{6,7},{7,6},{8,9},{9,8},{10,11... | collective-permute-start | bytes 86024 | tf_op jit(solution)/shard_map/ppermute | solution.py:520
  11.5 1.7 %copy-start = (f32[600,4,256]{2,1,0:T(4,128)S(1)}, f32[600,4,256]{2,1,0:T(4,128)}, u32[]{:S(2)}) copy-start(f32[600,4,256]{2,1,0:T(4,128)} %param.7) | copy-start | bytes 7372804
  13.2 10.1 %copy-start.1 = (f32[600,4,256]{2,1,0:T(4,128)S(1)}, f32[600,4,256]{2,1,0:T(4,128)}, u32[]{:S(2)}) copy-start(f32[600,4,256]{2,1,0:T(4,128)} %param.7) | copy-start | bytes 7372804
  13.5 13.6 %copy-start.4 = (f32[4,256]{1,0:T(4,128)S(1)}, f32[4,256]{1,0:T(4,128)}, u32[]{:S(2)}) copy-start(f32[4,256]{1,0:T(4,128)} %param.9) | copy-start | bytes 12292
  13.6 13.6 %copy-start.5 = (f32[4,256]{1,0:T(4,128)S(1)}, f32[4,256]{1,0:T(4,128)}, u32[]{:S(2)}) copy-start(f32[4,256]{1,0:T(4,128)} %param.10) | copy-start | bytes 12292
  13.6 13.6 %copy-start.6 = (s32[4,256]{1,0:T(4,128)S(1)}, s32[4,256]{1,0:T(4,128)}, u32[]{:S(2)}) copy-start(s32[4,256]{1,0:T(4,128)} %param.12) | copy-start | bytes 12292
  13.6 13.6 %copy-start.7 = (f32[25]{0:T(128)S(1)}, f32[25]{0:T(128)}, u32[]{:S(2)}) copy-start(f32[25]{0:T(128)} %constant.29.clone.ratio_ref) | copy-start | bytes 304
  14.5 14.9 %collective-permute-start.3 = (f32[157,8,128]{2,1,0:T(8,128)S(1)}, f32[157,8,128]{2,1,0:T(8,128)S(1)}, u32[]{:S(2)}, u32[]{:S(2)}) collective-permute-start(f32[157,8,128]{2,1,0:T(8,128)S(1)} %get-tuple-element.26), channel_id=1, source_target_pairs={{16,32},{32,16},{48,64},{64,48},{80,96},{96,80},{112,128},{128,112... | collective-permute-start | bytes 1929224 | tf_op jit(solution)/shard_map/ppermute | solution.py:524
  21.4 6.9 %collective-permute-start.2 = (f32[156,8,128]{2,1,0:T(8,128)S(1)}, f32[156,8,128]{2,1,0:T(8,128)S(1)}, u32[]{:S(2)}, u32[]{:S(2)}) collective-permute-start(f32[156,8,128]{2,1,0:T(8,128)S(1)} %shard_map.76), channel_id=1, source_target_pairs={{0,16},{16,0},{32,48},{48,32},{64,80},{80,64},{96,112},{112,96},{1... | collective-permute-start | bytes 1916936 | tf_op jit(solution)/shard_map/ppermute | solution.py:533

commit v3 on v2

--- a/solution.py
+++ b/solution.py
@@ -14,6 +14,7 @@
 LANES = 128
 PART = 5 * ND * 8
 PAD = 1
+PAIRED = 2
 PER = 5
 
 RATIO = np.float32(1.1) ** np.arange(NF, dtype=np.float32)
@@ -197,16 +198,16 @@
     lax.fori_loop(0, NF * 6 // 10, some, 0)
 
 
-def join_kernel(b_in, c_in, sea, even_ref, rows, out, rows_out):
+def join_kernel(second, first, sea, swap_ref, rows, out, rows_out):
     sub, lane = iotas()
     plus = packed_plus(sub, lane)
-    even = even_ref[0] == 1
+    swap = swap_ref[0] == 1
     for j in range(PER):
-        west = jnp.where(even, c_in[j], b_in[j])
-        east = jnp.where(even, b_in[j], c_in[j])
+        west = jnp.where(swap, second[j], first[j])
+        east = jnp.where(swap, first[j], second[j])
         out[j] = jnp.where(plus, west, east)
-    west = jnp.where(even, c_in[PER], b_in[PER])
-    east = jnp.where(even, b_in[PER + 1], c_in[PER + 1])
+    west = jnp.where(swap, second[PER], first[PER])
+    east = jnp.where(swap, first[PER + 1], second[PER + 1])
     out[PER] = jnp.where(plus, west, east)
     out[PER + 1] = sea[...].astype(jnp.float32)
     copy_rows(rows, rows_out)
@@ -507,20 +508,21 @@
     ns, nq = lax.axis_size("strip"), lax.axis_size("pt")
     pair_a = [(i, i ^ 1) for i in range(ns)]
     pair_z = [(i, ((i + 1) ^ 1) - 1) for i in range(1, ns - 1)]
-    pair_b = [(i, i ^ 1) for i in range(nq)]
-    pair_c = [(i, (((i + 1) ^ 1) - 1) % nq) for i in range(nq)]
+    paired = min(PAIRED, ns)
+    east_to = lambda s, p: (((p + 1) ^ 1) - 1) % nq if s < paired else (p + 1) % nq
+    west_to = lambda s, p: p ^ 1 if s < paired else (p - 1) % nq
+    turn = [[(s * nq + p, s * nq + to(s, p)) for s in range(ns) for p in range(nq)] for to in (east_to, west_to)]
     odd = (lax.axis_index("strip") % 2).reshape(1).astype(jnp.int32)
-    even = (1 - lax.axis_index("pt") % 2).reshape(1).astype(jnp.int32)
+    swap = ((lax.axis_index("strip") < paired) & (lax.axis_index("pt") % 2 == 1)).reshape(1).astype(jnp.int32)
     ratio = jnp.asarray(RATIO)
     spec = tiles(spectra).reshape(NF * ND * 8, LANES)
     wind_speed, wind_dir, sea, ice = (tiles(x) for x in (wind_speed, wind_dir, sea_mask, ice_mask))
     part_sems = pltpu.SemaphoreType.DMA((NF // PER + 1,))
     whole = pltpu.VMEM((NF * ND * 8, LANES), jnp.float32)
     xmsg = call(edges_kernel, REG(PER + 2), [HBM, HBM], [whole, pltpu.VMEM((8, LANES), jnp.int32), part_sems], cost=2.0, vmem=62 << 20)(spec, sea)
-    bin_ = lax.ppermute(xmsg, "pt", pair_b)
-    cin = lax.ppermute(xmsg, "pt", pair_c)
+    first, second = (lax.ppermute(xmsg, ("strip", "pt"), t) for t in turn)
     zrows, arows = call(rows_kernel, (REG(NF * 6), REG(NF * 6)), [VM, SM], cost=0.7)(spec, odd)
-    joined, zmsg = call(join_kernel, (REG(PER + 2), REG(NF * 6 + PER + 1 + PAD)), [VM, VM, VM, SM, VM], cost=0.2)(bin_, cin, sea, even, zrows)
+    joined, zmsg = call(join_kernel, (REG(PER + 2), REG(NF * 6 + PER + 1 + PAD)), [VM, VM, VM, SM, VM], cost=0.2)(second, first, sea, swap, zrows)
     zin = lax.ppermute(zmsg, "strip", pair_z)
     e2, mom = call(
         inner_kernel,

time: 32.2 us -> 30.5 us (0.947)
  starting transfers between devices: 17.4 us -> 16.5 us
  waiting for transfers between devices: 1.01 us -> 0.19 us
    ppermute x1, starting transfers between devices: 6.75 us -> 5.85 us  [on_device(): zin = lax.ppermute(zmsg, 'strip', pair_z)]
    ppermute x2, waiting for transfers between devices: 0.83 us -> 0.01 us  [on_device(): first, second = (lax.ppermute(xmsg, ('strip', 'pt'), t) for t in turn)]
  transfers between devices with their start and end apart: 4 -> 4, of which waited for: 2 -> 1; matrix products, arithmetic and copies ran while one was open for 0% -> 0% of each run, Pallas kernels for 19% -> 20%
where the time goes in v3:
time: 30.5 us; the launch traced here: 30.3 us
  starting transfers between devices  16.5 us (54%)
  Pallas kernels  11.6 us (38%)
  local copies, waits for them, and re-layouts  1.73 us (6%)
    ppermute x2, starting transfers between devices, on_device(): first, second = (lax.ppermute(xmsg, ('strip', 'pt'), t) for t in turn)  8.76 us
    ppermute x1, starting transfers between devices, on_device(): zin = lax.ppermute(zmsg, 'strip', pair_z)  5.85 us
    pallas_call x1, Pallas kernels, on_device(): call(inner_kernel, (REG(NF * 24), REG(16)), [VM, SM, VM, VM], [pltpu.VMEM...  3.81 us
    pallas_call x1, Pallas kernels, on_device(): call(edges_kernel, REG(PER + 2), [HBM, HBM], [whole, pltpu.VMEM((8, LANES...  2.73 us
    pallas_call x1, Pallas kernels, on_device(): call(outer_kernel, jax.ShapeDtypeStruct((NF * ND * 8, LANES), jnp.float32...  2.57 us
    ppermute x1, starting transfers between devices, on_device(): ain = lax.ppermute(amsg, 'strip', pair_a)  1.92 us
    unnamed x16, local copies, waits for them, and re-layouts  1.73 us
    pallas_call x1, Pallas kernels, on_device(): call(gain_kernel, (REG(NF * 24), REG(NF * 24)), [SM, VM, VM, VM, VM], [pl...  1.08 us
  transfers between devices with their start and end apart: 4, of which 1 were waited for; matrix products, arithmetic and copies ran while one was open for 0% of the time, Pallas kernels for 20%

profile of v3, /device:TPU:225, one launch (start us, length us, event | category | flops | bytes accessed | tf_op | source)
XLA Modules:
  0.0 30.3 jit_solution(7698042796932025735)
XLA Ops:
  0.0 0.0 copy-start.2
  0.0 2.7 %shard_map.74 = f32[7,8,128]{2,1,0:T(8,128)} custom-call(f32[4800,128]{1,0:T(8,128)} %bitcast.32, s32[8,128]{1,0:T(8,128)} %bitcast.35), custom_call_target="tpu_custom_call" | custom-call | bytes 7200000 | tf_op jit(solution)/shard_map/pallas_call | solution.py:522
  2.7 0.0 copy-start.3
  2.8 3.2 %collective-permute-start.1 = (f32[7,8,128]{2,1,0:T(8,128)}, f32[7,8,128]{2,1,0:T(8,128)S(1)}, u32[]{:S(2)}, u32[]{:S(2)}) collective-permute-start(f32[7,8,128]{2,1,0:T(8,128)} %shard_map.74), channel_id=1, source_target_pairs={{0,15},{1,2},{2,1},{3,4},{4,3},{5,6},{6,5},{7,8},{8,7},{9,10},{10,... | collective-permute-start | bytes 86024 | tf_op jit(solution)/shard_map/ppermute | solution.py:523
  6.0 5.6 %collective-permute-start = (f32[7,8,128]{2,1,0:T(8,128)}, f32[7,8,128]{2,1,0:T(8,128)S(1)}, u32[]{:S(2)}, u32[]{:S(2)}) collective-permute-start(f32[7,8,128]{2,1,0:T(8,128)} %shard_map.74), channel_id=1, source_target_pairs={{0,1},{1,0},{2,3},{3,2},{4,5},{5,4},{6,7},{7,6},{8,9},{9,8},{10,11... | collective-permute-start | bytes 86024 | tf_op jit(solution)/shard_map/ppermute | solution.py:523
  11.6 0.0 copy-start
  11.6 1.7 %copy-done = f32[600,4,256]{2,1,0:T(4,128)S(1)} copy-done((f32[600,4,256]{2,1,0:T(4,128)S(1)}, f32[600,4,256]{2,1,0:T(4,128)}, u32[]{:S(2)}) %copy-start) | copy-done | bytes 2457624
  13.2 0.0 copy-start.1
  13.2 0.3 shard_map.73
  13.5 0.0 copy-start.4
  13.6 0.0 copy-start.5
  13.6 0.0 copy-start.6
  13.6 0.0 copy-start.7
  13.6 0.0 collective-permute-done.1.first
  13.6 0.0 collective-permute-done.second
  13.6 0.0 copy-done.2
  13.6 0.1 shard_map.75
  13.7 5.9 %collective-permute-start.3 = (f32[157,8,128]{2,1,0:T(8,128)S(1)}, f32[157,8,128]{2,1,0:T(8,128)S(1)}, u32[]{:S(2)}, u32[]{:S(2)}) collective-permute-start(f32[157,8,128]{2,1,0:T(8,128)S(1)} %get-tuple-element.26), channel_id=1, source_target_pairs={{16,32},{32,16},{48,64},{64,48},{80,96},{96,80},{112,128},{128,112... | collective-permute-start | bytes 1929224 | tf_op jit(solution)/shard_map/ppermute | solution.py:526
  19.6 0.1 shard_map.76
  19.7 1.9 %collective-permute-start.2 = (f32[156,8,128]{2,1,0:T(8,128)S(1)}, f32[156,8,128]{2,1,0:T(8,128)S(1)}, u32[]{:S(2)}, u32[]{:S(2)}) collective-permute-start(f32[156,8,128]{2,1,0:T(8,128)S(1)} %shard_map.76), channel_id=1, source_target_pairs={{0,16},{16,0},{32,48},{48,32},{64,80},{80,64},{96,112},{112,96},{1... | collective-permute-start | bytes 1916936 | tf_op jit(solution)/shard_map/ppermute | solution.py:535
  21.6 0.0 copy-done.3
  21.6 0.0 copy-done.1
  21.6 3.8 %shard_map.77 = (f32[600,8,128]{2,1,0:T(8,128)S(1)}, f32[16,8,128]{2,1,0:T(8,128)S(1)}) custom-call(f32[4800,128]{1,0:T(8,128)S(1)} %bitcast.34, f32[25]{0:T(128)S(1)} %copy-done.3, s32[8,128]{1,0:T(8,128)S(1)} %bitcast.37, f32[7,8,128]{2,1,0:T(8,128)S(1)} %get-tuple-element.18.joined), custom_call_target="tpu_custom_call" | custom-call | bytes 18000000 | tf_op jit(solution)/shard_map/pallas_call | solution.py:527
  25.5 0.0 copy-done.4
  25.5 0.0 copy-done.5
  25.5 0.0 copy-done.6
  25.5 0.0 copy-done.7
  25.5 1.1 %shard_map.78 = (f32[600,8,128]{2,1,0:T(8,128)S(1)}, f32[600,8,128]{2,1,0:T(8,128)S(1)}) custom-call(f32[25]{0:T(128)S(1)} %copy-done.7, f32[8,128]{1,0:T(8,128)S(1)} %bitcast.38, f32[8,128]{1,0:T(8,128)S(1)} %bitcast.39, s32[8,128]{1,0:T(8,128)S(1)} %bitcast.40, f32[600,8,128]{2,1,0:T(8,128)S(1)} %get-tuple-element.20.e_in), custom_call_target="tpu_custom_call" | custom-call | bytes 3600000 | tf_op jit(solution)/shard_map/pallas_call | solution.py:537
  26.6 0.0 collective-permute-done.2.a_in
  26.6 0.9 %shard_map.79 = (f32[200,8,128]{2,1,0:T(8,128)S(1)}, f32[16,8,128]{2,1,0:T(8,128)S(1)}) custom-call(f32[25]{0:T(128)S(1)} %copy-done.3, s32[1]{0:T(128)} %bitcast.odd_ref, f32[600,8,128]{2,1,0:T(8,128)S(1)} %get-tuple-element.22.f, f32[16,8,128]{2,1,0:T(8,128)S(1)} %get-tuple-element.23.mom, f32[156,8,128]{2,1,0:T(8,128)S(1)} %collective-permute-done.2.a_in, ...), custom_call_target="tpu_custom_call" | custom-call | tf_op jit(solution)/shard_map/pallas_call | solution.py:540
  27.5 0.2 collective-permute-done.3.z_in
  27.7 2.6 %shard_map.80 = f32[4800,128]{1,0:T(8,128)} custom-call(f32[25]{0:T(128)S(1)} %copy-done.3, s32[1]{0:T(128)} %bitcast.odd_ref, f32[600,8,128]{2,1,0:T(8,128)S(1)} %get-tuple-element.21.pf, f32[600,8,128]{2,1,0:T(8,128)S(1)} %get-tuple-element.22.f, f32[16,8,128]{2,1,0:T(8,128)S(1)} %get-tuple-element.24.mom, f32[200,8,128]{2,1,0:T(8,128)S(1)} %get-tuple-element.25.near, ...), custom_call_target="tpu_custom_call" | custom-call | bytes 10800000 | tf_op jit(solution)/shard_map/pallas_call | solution.py:541
Async XLA Ops:
  0.0 13.6 %copy-start.2 = (s32[4,256]{1,0:T(4,128)S(1)}, s32[4,256]{1,0:T(4,128)}, u32[]{:S(2)}) copy-start(s32[4,256]{1,0:T(4,128)} %param.11) | copy-start | bytes 12292
  2.7 18.9 %copy-start.3 = (f32[25]{0:T(128)S(1)}, f32[25]{0:T(128)}, u32[]{:S(2)}) copy-start(f32[25]{0:T(128)} %courant.5) | copy-start | bytes 304
  2.8 10.8 %collective-permute-start.1 = (f32[7,8,128]{2,1,0:T(8,128)}, f32[7,8,128]{2,1,0:T(8,128)S(1)}, u32[]{:S(2)}, u32[]{:S(2)}) collective-permute-start(f32[7,8,128]{2,1,0:T(8,128)} %shard_map.74), channel_id=1, source_target_pairs={{0,15},{1,2},{2,1},{3,4},{4,3},{5,6},{6,5},{7,8},{8,7},{9,10},{10,... | collective-permute-start | bytes 86024 | tf_op jit(solution)/shard_map/ppermute | solution.py:523
  6.0 7.6 %collective-permute-start = (f32[7,8,128]{2,1,0:T(8,128)}, f32[7,8,128]{2,1,0:T(8,128)S(1)}, u32[]{:S(2)}, u32[]{:S(2)}) collective-permute-start(f32[7,8,128]{2,1,0:T(8,128)} %shard_map.74), channel_id=1, source_target_pairs={{0,1},{1,0},{2,3},{3,2},{4,5},{5,4},{6,7},{7,6},{8,9},{9,8},{10,11... | collective-permute-start | bytes 86024 | tf_op jit(solution)/shard_map/ppermute | solution.py:523
  11.6 1.7 %copy-start = (f32[600,4,256]{2,1,0:T(4,128)S(1)}, f32[600,4,256]{2,1,0:T(4,128)}, u32[]{:S(2)}) copy-start(f32[600,4,256]{2,1,0:T(4,128)} %param.7) | copy-start | bytes 7372804
  13.2 8.4 %copy-start.1 = (f32[600,4,256]{2,1,0:T(4,128)S(1)}, f32[600,4,256]{2,1,0:T(4,128)}, u32[]{:S(2)}) copy-start(f32[600,4,256]{2,1,0:T(4,128)} %param.7) | copy-start | bytes 7372804
  13.5 11.9 %copy-start.4 = (f32[4,256]{1,0:T(4,128)S(1)}, f32[4,256]{1,0:T(4,128)}, u32[]{:S(2)}) copy-start(f32[4,256]{1,0:T(4,128)} %param.9) | copy-start | bytes 12292
  13.6 11.9 %copy-start.5 = (f32[4,256]{1,0:T(4,128)S(1)}, f32[4,256]{1,0:T(4,128)}, u32[]{:S(2)}) copy-start(f32[4,256]{1,0:T(4,128)} %param.10) | copy-start | bytes 12292
  13.6 11.9 %copy-start.6 = (s32[4,256]{1,0:T(4,128)S(1)}, s32[4,256]{1,0:T(4,128)}, u32[]{:S(2)}) copy-start(s32[4,256]{1,0:T(4,128)} %param.12) | copy-start | bytes 12292
  13.6 11.9 %copy-start.7 = (f32[25]{0:T(128)S(1)}, f32[25]{0:T(128)}, u32[]{:S(2)}) copy-start(f32[25]{0:T(128)} %constant.29.clone.ratio_ref) | copy-start | bytes 304
  13.7 14.0 %collective-permute-start.3 = (f32[157,8,128]{2,1,0:T(8,128)S(1)}, f32[157,8,128]{2,1,0:T(8,128)S(1)}, u32[]{:S(2)}, u32[]{:S(2)}) collective-permute-start(f32[157,8,128]{2,1,0:T(8,128)S(1)} %get-tuple-element.26), channel_id=1, source_target_pairs={{16,32},{32,16},{48,64},{64,48},{80,96},{96,80},{112,128},{128,112... | collective-permute-start | bytes 1929224 | tf_op jit(solution)/shard_map/ppermute | solution.py:526
  19.7 6.9 %collective-permute-start.2 = (f32[156,8,128]{2,1,0:T(8,128)S(1)}, f32[156,8,128]{2,1,0:T(8,128)S(1)}, u32[]{:S(2)}, u32[]{:S(2)}) collective-permute-start(f32[156,8,128]{2,1,0:T(8,128)S(1)} %shard_map.76), channel_id=1, source_target_pairs={{0,16},{16,0},{32,48},{48,32},{64,80},{80,64},{96,112},{112,96},{1... | collective-permute-start | bytes 1916936 | tf_op jit(solution)/shard_map/ppermute | solution.py:535

commit v4 on v3

--- a/solution.py
+++ b/solution.py
@@ -114,23 +114,13 @@
     return x
 
 
-def edges_kernel(spec_hbm, sea_hbm, x_out, spec, sea, sems):
+def edges_kernel(spec, sea, x_out):
     sub, lane = iotas()
-
-    def fetch(block):
-        part = pl.ds(block * PART, PART)
-        return pltpu.make_async_copy(spec_hbm.at[part], spec.at[part], sems.at[block])
-
-    sea_copy = pltpu.make_async_copy(sea_hbm, sea, sems.at[NF // PER])
-    sea_copy.start()
-    for block in range(NF // PER):
-        fetch(block).start()
     here = lane // 2
     shifted = ((lane + 2) & (LANES - 1)) // 2
     plus_at = packed_plus(sub, lane)
 
-    sea_copy.wait()
-    seaf = sea[...].astype(jnp.float32)
+    seaf = sea[...]
     slot_e = jnp.zeros((8, LANES), jnp.float32)
     slot_w = jnp.zeros((8, LANES), jnp.float32)
     for r in range(ROWS):
@@ -143,7 +133,6 @@
     x_out[PER + 1] = spread(slot_w, lane)
 
     for block in range(NF // PER):
-        fetch(block).wait()
         zero = jnp.zeros((8, LANES), jnp.float32)
         easts, wests = [zero] * 3, [zero] * 3
         for t in range(PER):
@@ -209,7 +198,7 @@
     west = jnp.where(swap, second[PER], first[PER])
     east = jnp.where(swap, first[PER + 1], second[PER + 1])
     out[PER] = jnp.where(plus, west, east)
-    out[PER + 1] = sea[...].astype(jnp.float32)
+    out[PER + 1] = sea[...]
     copy_rows(rows, rows_out)
     for j in range(PER):
         rows_out[NF * 6 + j] = out[j]
@@ -261,7 +250,7 @@
 def inner_kernel(spec, courant, sea, joined, e_out, mom_out, edge2):
     sub, lane = iotas()
     cu, cv = direction_tables(sub)
-    seaf = sea[...].astype(jnp.float32)
+    seaf = sea[...]
     slot = lane // 8
     group = slot % NG
     rr = (lane % 8) // 2
@@ -516,10 +505,10 @@
     swap = ((lax.axis_index("strip") < paired) & (lax.axis_index("pt") % 2 == 1)).reshape(1).astype(jnp.int32)
     ratio = jnp.asarray(RATIO)
     spec = tiles(spectra).reshape(NF * ND * 8, LANES)
-    wind_speed, wind_dir, sea, ice = (tiles(x) for x in (wind_speed, wind_dir, sea_mask, ice_mask))
+    wind_speed, wind_dir, sea, ice = (tiles(x) for x in (wind_speed, wind_dir, sea_mask.astype(jnp.float32), ice_mask))
     part_sems = pltpu.SemaphoreType.DMA((NF // PER + 1,))
     whole = pltpu.VMEM((NF * ND * 8, LANES), jnp.float32)
-    xmsg = call(edges_kernel, REG(PER + 2), [HBM, HBM], [whole, pltpu.VMEM((8, LANES), jnp.int32), part_sems], cost=2.0, vmem=62 << 20)(spec, sea)
+    xmsg = call(edges_kernel, REG(PER + 2), [VM, VM], cost=1.0)(spec, sea)
     first, second = (lax.ppermute(xmsg, ("strip", "pt"), t) for t in turn)
     zrows, arows = call(rows_kernel, (REG(NF * 6), REG(NF * 6)), [VM, SM], cost=0.7)(spec, odd)
     joined, zmsg = call(join_kernel, (REG(PER + 2), REG(NF * 6 + PER + 1 + PAD)), [VM, VM, VM, SM, VM], cost=0.2)(second, first, sea, swap, zrows)

time: 30.5 us -> 30.6 us (level)
  the two profiles are of different devices: /device:TPU:225 before, /device:TPU:255 now
where the time goes in v4:
time: 30.6 us; the launch traced here: 30.4 us
  starting transfers between devices  13.9 us (45%)
  Pallas kernels  9.42 us (31%)
  waiting for transfers between devices  4.41 us (14%)
  local copies, waits for them, and re-layouts  1.73 us (6%)
  other arithmetic  0.69 us (2%)
    ppermute x1, starting transfers between devices, on_device(): zin = lax.ppermute(zmsg, 'strip', pair_z)  6.59 us
    ppermute x2, starting transfers between devices, on_device(): first, second = (lax.ppermute(xmsg, ('strip', 'pt'), t) for t in turn)  5.41 us
    ppermute x2, waiting for transfers between devices, on_device(): first, second = (lax.ppermute(xmsg, ('strip', 'pt'), t) for t in turn)  4.17 us
    pallas_call x1, Pallas kernels, on_device(): call(inner_kernel, (REG(NF * 24), REG(16)), [VM, SM, VM, VM], [pltpu.VMEM...  3.8 us
    pallas_call x1, Pallas kernels, on_device(): call(outer_kernel, jax.ShapeDtypeStruct((NF * ND * 8, LANES), jnp.float32...  2.55 us
    ppermute x1, starting transfers between devices, on_device(): ain = lax.ppermute(amsg, 'strip', pair_a)  1.92 us
    unnamed x14, local copies, waits for them, and re-layouts  1.73 us
    pallas_call x1, Pallas kernels, on_device(): call(gain_kernel, (REG(NF * 24), REG(NF * 24)), [SM, VM, VM, VM, VM], [pl...  1.06 us
  transfers between devices with their start and end apart: 4, of which 2 were waited for; matrix products, arithmetic and copies ran while one was open for 0% of the time, Pallas kernels for 20%

profile of v4, /device:TPU:255, one launch (start us, length us, event | category | flops | bytes accessed | tf_op | source)
XLA Modules:
  0.0 30.4 jit_solution(8804288618997501623)
XLA Ops:
  0.0 0.7 %convert_element_type.8 = f32[4,256]{1,0:T(4,128)S(1)} convert(s32[4,256]{1,0:T(4,128)} %param.11) | non-fusion elementwise | flops 1024 | bytes 8192 | tf_op jit(solution)/shard_map/convert_element_type | solution.py:508
  0.7 0.0 copy-start
  0.7 1.7 %copy-done = f32[600,4,256]{2,1,0:T(4,128)S(1)} copy-done((f32[600,4,256]{2,1,0:T(4,128)S(1)}, f32[600,4,256]{2,1,0:T(4,128)}, u32[]{:S(2)}) %copy-start) | copy-done | bytes 2457624
  2.4 0.0 copy-start.1
  2.4 0.6 %shard_map.74 = f32[7,8,128]{2,1,0:T(8,128)S(1)} custom-call(f32[4800,128]{1,0:T(8,128)S(1)} %bitcast.32, f32[8,128]{1,0:T(8,128)S(1)} %bitcast.35), custom_call_target="tpu_custom_call" | custom-call | bytes 3600000 | tf_op jit(solution)/shard_map/pallas_call | solution.py:511
  3.0 0.0 copy-start.2
  3.0 2.0 %collective-permute-start.1 = (f32[7,8,128]{2,1,0:T(8,128)S(1)}, f32[7,8,128]{2,1,0:T(8,128)S(1)}, u32[]{:S(2)}, u32[]{:S(2)}) collective-permute-start(f32[7,8,128]{2,1,0:T(8,128)S(1)} %shard_map.74), channel_id=1, source_target_pairs={{0,15},{1,2},{2,1},{3,4},{4,3},{5,6},{6,5},{7,8},{8,7},{9,10},{10,... | collective-permute-start | bytes 86024 | tf_op jit(solution)/shard_map/ppermute | solution.py:512
  5.1 3.4 %collective-permute-start = (f32[7,8,128]{2,1,0:T(8,128)S(1)}, f32[7,8,128]{2,1,0:T(8,128)S(1)}, u32[]{:S(2)}, u32[]{:S(2)}) collective-permute-start(f32[7,8,128]{2,1,0:T(8,128)S(1)} %shard_map.74), channel_id=1, source_target_pairs={{0,1},{1,0},{2,3},{3,2},{4,5},{5,4},{6,7},{7,6},{8,9},{9,8},{10,11... | collective-permute-start | bytes 86024 | tf_op jit(solution)/shard_map/ppermute | solution.py:512
  8.5 0.0 copy-done.1
  8.5 0.3 shard_map.73
  8.8 0.0 copy-start.3
  8.8 0.0 copy-start.4
  8.8 0.0 copy-start.5
  8.8 0.0 copy-start.6
  8.8 0.0 collective-permute-done.1.first
  8.8 4.2 %collective-permute-done.second = f32[7,8,128]{2,1,0:T(8,128)S(1)} collective-permute-done((f32[7,8,128]{2,1,0:T(8,128)S(1)}, f32[7,8,128]{2,1,0:T(8,128)S(1)}, u32[]{:S(2)}, u32[]{:S(2)}) %collective-permute-start) | collective-permute-done | bytes 28704 | tf_op jit(solution)/shard_map/ppermute | solution.py:512
  13.0 0.1 shard_map.75
  13.1 6.6 %collective-permute-start.3 = (f32[157,8,128]{2,1,0:T(8,128)S(1)}, f32[157,8,128]{2,1,0:T(8,128)S(1)}, u32[]{:S(2)}, u32[]{:S(2)}) collective-permute-start(f32[157,8,128]{2,1,0:T(8,128)S(1)} %get-tuple-element.26), channel_id=1, source_target_pairs={{16,32},{32,16},{48,64},{64,48},{80,96},{96,80},{112,128},{128,112... | collective-permute-start | bytes 1929224 | tf_op jit(solution)/shard_map/ppermute | solution.py:515
  19.7 0.1 shard_map.76
  19.8 1.9 %collective-permute-start.2 = (f32[156,8,128]{2,1,0:T(8,128)S(1)}, f32[156,8,128]{2,1,0:T(8,128)S(1)}, u32[]{:S(2)}, u32[]{:S(2)}) collective-permute-start(f32[156,8,128]{2,1,0:T(8,128)S(1)} %shard_map.76), channel_id=1, source_target_pairs={{0,16},{16,0},{32,48},{48,32},{64,80},{80,64},{96,112},{112,96},{1... | collective-permute-start | bytes 1916936 | tf_op jit(solution)/shard_map/ppermute | solution.py:524
  21.7 0.0 copy-done.2
  21.7 3.8 %shard_map.77 = (f32[600,8,128]{2,1,0:T(8,128)S(1)}, f32[16,8,128]{2,1,0:T(8,128)S(1)}) custom-call(f32[4800,128]{1,0:T(8,128)S(1)} %bitcast.34, f32[25]{0:T(128)S(1)} %copy-done.2, f32[8,128]{1,0:T(8,128)S(1)} %bitcast.37, f32[7,8,128]{2,1,0:T(8,128)S(1)} %get-tuple-element.18.joined), custom_call_target="tpu_custom_call" | custom-call | bytes 18000000 | tf_op jit(solution)/shard_map/pallas_call | solution.py:516
  25.5 0.0 copy-done.3
  25.5 0.0 copy-done.4
  25.6 0.0 copy-done.5
  25.6 0.0 copy-done.6
  25.6 1.1 %shard_map.78 = (f32[600,8,128]{2,1,0:T(8,128)S(1)}, f32[600,8,128]{2,1,0:T(8,128)S(1)}) custom-call(f32[25]{0:T(128)S(1)} %copy-done.6, f32[8,128]{1,0:T(8,128)S(1)} %bitcast.38, f32[8,128]{1,0:T(8,128)S(1)} %bitcast.39, s32[8,128]{1,0:T(8,128)S(1)} %bitcast.40, f32[600,8,128]{2,1,0:T(8,128)S(1)} %get-tuple-element.20.e_in), custom_call_target="tpu_custom_call" | custom-call | bytes 3600000 | tf_op jit(solution)/shard_map/pallas_call | solution.py:526
  26.6 0.0 collective-permute-done.2.a_in
  26.7 0.9 %shard_map.79 = (f32[200,8,128]{2,1,0:T(8,128)S(1)}, f32[16,8,128]{2,1,0:T(8,128)S(1)}) custom-call(f32[25]{0:T(128)S(1)} %copy-done.2, s32[1]{0:T(128)} %bitcast.odd_ref, f32[600,8,128]{2,1,0:T(8,128)S(1)} %get-tuple-element.22.f, f32[16,8,128]{2,1,0:T(8,128)S(1)} %get-tuple-element.23.mom, f32[156,8,128]{2,1,0:T(8,128)S(1)} %collective-permute-done.2.a_in, ...), custom_call_target="tpu_custom_call" | custom-call | tf_op jit(solution)/shard_map/pallas_call | solution.py:529
  27.6 0.2 collective-permute-done.3.z_in
  27.8 2.5 %shard_map.80 = f32[4800,128]{1,0:T(8,128)} custom-call(f32[25]{0:T(128)S(1)} %copy-done.2, s32[1]{0:T(128)} %bitcast.odd_ref, f32[600,8,128]{2,1,0:T(8,128)S(1)} %get-tuple-element.21.pf, f32[600,8,128]{2,1,0:T(8,128)S(1)} %get-tuple-element.22.f, f32[16,8,128]{2,1,0:T(8,128)S(1)} %get-tuple-element.24.mom, f32[200,8,128]{2,1,0:T(8,128)S(1)} %get-tuple-element.25.near, ...), custom_call_target="tpu_custom_call" | custom-call | bytes 10800000 | tf_op jit(solution)/shard_map/pallas_call | solution.py:530
Async XLA Ops:
  0.7 1.7 %copy-start = (f32[600,4,256]{2,1,0:T(4,128)S(1)}, f32[600,4,256]{2,1,0:T(4,128)}, u32[]{:S(2)}) copy-start(f32[600,4,256]{2,1,0:T(4,128)} %param.7) | copy-start | bytes 7372804
  2.4 6.1 %copy-start.1 = (f32[600,4,256]{2,1,0:T(4,128)S(1)}, f32[600,4,256]{2,1,0:T(4,128)}, u32[]{:S(2)}) copy-start(f32[600,4,256]{2,1,0:T(4,128)} %param.7) | copy-start | bytes 7372804
  3.0 18.7 %copy-start.2 = (f32[25]{0:T(128)S(1)}, f32[25]{0:T(128)}, u32[]{:S(2)}) copy-start(f32[25]{0:T(128)} %courant.5) | copy-start | bytes 304
  3.0 5.8 %collective-permute-start.1 = (f32[7,8,128]{2,1,0:T(8,128)S(1)}, f32[7,8,128]{2,1,0:T(8,128)S(1)}, u32[]{:S(2)}, u32[]{:S(2)}) collective-permute-start(f32[7,8,128]{2,1,0:T(8,128)S(1)} %shard_map.74), channel_id=1, source_target_pairs={{0,15},{1,2},{2,1},{3,4},{4,3},{5,6},{6,5},{7,8},{8,7},{9,10},{10,... | collective-permute-start | bytes 86024 | tf_op jit(solution)/shard_map/ppermute | solution.py:512
  5.1 7.9 %collective-permute-start = (f32[7,8,128]{2,1,0:T(8,128)S(1)}, f32[7,8,128]{2,1,0:T(8,128)S(1)}, u32[]{:S(2)}, u32[]{:S(2)}) collective-permute-start(f32[7,8,128]{2,1,0:T(8,128)S(1)} %shard_map.74), channel_id=1, source_target_pairs={{0,1},{1,0},{2,3},{3,2},{4,5},{5,4},{6,7},{7,6},{8,9},{9,8},{10,11... | collective-permute-start | bytes 86024 | tf_op jit(solution)/shard_map/ppermute | solution.py:512
  8.8 16.8 %copy-start.3 = (f32[4,256]{1,0:T(4,128)S(1)}, f32[4,256]{1,0:T(4,128)}, u32[]{:S(2)}) copy-start(f32[4,256]{1,0:T(4,128)} %param.9) | copy-start | bytes 12292
  8.8 16.8 %copy-start.4 = (f32[4,256]{1,0:T(4,128)S(1)}, f32[4,256]{1,0:T(4,128)}, u32[]{:S(2)}) copy-start(f32[4,256]{1,0:T(4,128)} %param.10) | copy-start | bytes 12292
  8.8 16.8 %copy-start.5 = (s32[4,256]{1,0:T(4,128)S(1)}, s32[4,256]{1,0:T(4,128)}, u32[]{:S(2)}) copy-start(s32[4,256]{1,0:T(4,128)} %param.12) | copy-start | bytes 12292
  8.8 16.8 %copy-start.6 = (f32[25]{0:T(128)S(1)}, f32[25]{0:T(128)}, u32[]{:S(2)}) copy-start(f32[25]{0:T(128)} %constant.29.clone.ratio_ref) | copy-start | bytes 304
  13.1 14.7 %collective-permute-start.3 = (f32[157,8,128]{2,1,0:T(8,128)S(1)}, f32[157,8,128]{2,1,0:T(8,128)S(1)}, u32[]{:S(2)}, u32[]{:S(2)}) collective-permute-start(f32[157,8,128]{2,1,0:T(8,128)S(1)} %get-tuple-element.26), channel_id=1, source_target_pairs={{16,32},{32,16},{48,64},{64,48},{80,96},{96,80},{112,128},{128,112... | collective-permute-start | bytes 1929224 | tf_op jit(solution)/shard_map/ppermute | solution.py:515
  19.8 6.9 %collective-permute-start.2 = (f32[156,8,128]{2,1,0:T(8,128)S(1)}, f32[156,8,128]{2,1,0:T(8,128)S(1)}, u32[]{:S(2)}, u32[]{:S(2)}) collective-permute-start(f32[156,8,128]{2,1,0:T(8,128)S(1)} %shard_map.76), channel_id=1, source_target_pairs={{0,16},{16,0},{32,48},{48,32},{64,80},{80,64},{96,112},{112,96},{1... | collective-permute-start | bytes 1916936 | tf_op jit(solution)/shard_map/ppermute | solution.py:524

commit v5 on v4

--- a/solution.py
+++ b/solution.py
@@ -129,8 +129,7 @@
         place = lane // 2 == r
         slot_e = jnp.where(place, last, slot_e)
         slot_w = jnp.where(place, first, slot_w)
-    x_out[PER] = spread(slot_e, lane)
-    x_out[PER + 1] = spread(slot_w, lane)
+    x_out[PER] = jnp.where(plus_at, spread(slot_e, lane), spread(slot_w, lane))
 
     for block in range(NF // PER):
         zero = jnp.zeros((8, LANES), jnp.float32)
@@ -196,7 +195,7 @@
         east = jnp.where(swap, first[j], second[j])
         out[j] = jnp.where(plus, west, east)
     west = jnp.where(swap, second[PER], first[PER])
-    east = jnp.where(swap, first[PER + 1], second[PER + 1])
+    east = jnp.where(swap, first[PER], second[PER])
     out[PER] = jnp.where(plus, west, east)
     out[PER + 1] = sea[...]
     copy_rows(rows, rows_out)
@@ -508,7 +507,7 @@
     wind_speed, wind_dir, sea, ice = (tiles(x) for x in (wind_speed, wind_dir, sea_mask.astype(jnp.float32), ice_mask))
     part_sems = pltpu.SemaphoreType.DMA((NF // PER + 1,))
     whole = pltpu.VMEM((NF * ND * 8, LANES), jnp.float32)
-    xmsg = call(edges_kernel, REG(PER + 2), [VM, VM], cost=1.0)(spec, sea)
+    xmsg = call(edges_kernel, REG(PER + 1), [VM, VM], cost=1.0)(spec, sea)
     first, second = (lax.ppermute(xmsg, ("strip", "pt"), t) for t in turn)
     zrows, arows = call(rows_kernel, (REG(NF * 6), REG(NF * 6)), [VM, SM], cost=0.7)(spec, odd)
     joined, zmsg = call(join_kernel, (REG(PER + 2), REG(NF * 6 + PER + 1 + PAD)), [VM, VM, VM, SM, VM], cost=0.2)(second, first, sea, swap, zrows)

time: 30.6 us -> 30.6 us (level)
  the two profiles are of different devices: /device:TPU:255 before, /device:TPU:127 now
where the time goes in v5:
time: 30.6 us; the launch traced here: 30.3 us
  starting transfers between devices  13.9 us (45%)
  Pallas kernels  9.42 us (31%)
  waiting for transfers between devices  4.37 us (14%)
  local copies, waits for them, and re-layouts  1.73 us (6%)
  other arithmetic  0.69 us (2%)
    ppermute x1, starting transfers between devices, on_device(): zin = lax.ppermute(zmsg, 'strip', pair_z)  6.59 us
    ppermute x2, starting transfers between devices, on_device(): first, second = (lax.ppermute(xmsg, ('strip', 'pt'), t) for t in turn)  5.41 us
    ppermute x2, waiting for transfers between devices, on_device(): first, second = (lax.ppermute(xmsg, ('strip', 'pt'), t) for t in turn)  4.13 us
    pallas_call x1, Pallas kernels, on_device(): call(inner_kernel, (REG(NF * 24), REG(16)), [VM, SM, VM, VM], [pltpu.VMEM...  3.8 us
    pallas_call x1, Pallas kernels, on_device(): call(outer_kernel, jax.ShapeDtypeStruct((NF * ND * 8, LANES), jnp.float32...  2.55 us
    ppermute x1, starting transfers between devices, on_device(): ain = lax.ppermute(amsg, 'strip', pair_a)  1.92 us
    unnamed x14, local copies, waits for them, and re-layouts  1.73 us
    pallas_call x1, Pallas kernels, on_device(): call(gain_kernel, (REG(NF * 24), REG(NF * 24)), [SM, VM, VM, VM, VM], [pl...  1.06 us
  transfers between devices with their start and end apart: 4, of which 2 were waited for; matrix products, arithmetic and copies ran while one was open for 0% of the time, Pallas kernels for 20%

profile of v5, /device:TPU:127, one launch (start us, length us, event | category | flops | bytes accessed | tf_op | source)
XLA Modules:
  0.0 30.3 jit_solution(9663938915791655064)
XLA Ops:
  0.0 0.7 %convert_element_type.8 = f32[4,256]{1,0:T(4,128)S(1)} convert(s32[4,256]{1,0:T(4,128)} %param.11) | non-fusion elementwise | flops 1024 | bytes 8192 | tf_op jit(solution)/shard_map/convert_element_type | solution.py:507
  0.7 0.0 copy-start
  0.7 1.7 %copy-done = f32[600,4,256]{2,1,0:T(4,128)S(1)} copy-done((f32[600,4,256]{2,1,0:T(4,128)S(1)}, f32[600,4,256]{2,1,0:T(4,128)}, u32[]{:S(2)}) %copy-start) | copy-done | bytes 2457624
  2.4 0.0 copy-start.1
  2.4 0.6 %shard_map.74 = f32[6,8,128]{2,1,0:T(8,128)S(1)} custom-call(f32[4800,128]{1,0:T(8,128)S(1)} %bitcast.32, f32[8,128]{1,0:T(8,128)S(1)} %bitcast.35), custom_call_target="tpu_custom_call" | custom-call | bytes 3600000 | tf_op jit(solution)/shard_map/pallas_call | solution.py:510
  3.0 0.0 copy-start.2
  3.0 2.0 %collective-permute-start.1 = (f32[6,8,128]{2,1,0:T(8,128)S(1)}, f32[6,8,128]{2,1,0:T(8,128)S(1)}, u32[]{:S(2)}, u32[]{:S(2)}) collective-permute-start(f32[6,8,128]{2,1,0:T(8,128)S(1)} %shard_map.74), channel_id=1, source_target_pairs={{0,15},{1,2},{2,1},{3,4},{4,3},{5,6},{6,5},{7,8},{8,7},{9,10},{10,... | collective-permute-start | bytes 73736 | tf_op jit(solution)/shard_map/ppermute | solution.py:511
  5.1 3.4 %collective-permute-start = (f32[6,8,128]{2,1,0:T(8,128)S(1)}, f32[6,8,128]{2,1,0:T(8,128)S(1)}, u32[]{:S(2)}, u32[]{:S(2)}) collective-permute-start(f32[6,8,128]{2,1,0:T(8,128)S(1)} %shard_map.74), channel_id=1, source_target_pairs={{0,1},{1,0},{2,3},{3,2},{4,5},{5,4},{6,7},{7,6},{8,9},{9,8},{10,11... | collective-permute-start | bytes 73736 | tf_op jit(solution)/shard_map/ppermute | solution.py:511
  8.5 0.0 copy-done.1
  8.5 0.3 shard_map.73
  8.8 0.0 copy-start.3
  8.8 0.0 copy-start.4
  8.8 0.0 copy-start.5
  8.8 0.0 copy-start.6
  8.8 0.0 collective-permute-done.1.first
  8.8 4.1 %collective-permute-done.second = f32[6,8,128]{2,1,0:T(8,128)S(1)} collective-permute-done((f32[6,8,128]{2,1,0:T(8,128)S(1)}, f32[6,8,128]{2,1,0:T(8,128)S(1)}, u32[]{:S(2)}, u32[]{:S(2)}) %collective-permute-start) | collective-permute-done | bytes 24608 | tf_op jit(solution)/shard_map/ppermute | solution.py:511
  13.0 0.1 shard_map.75
  13.1 6.6 %collective-permute-start.3 = (f32[157,8,128]{2,1,0:T(8,128)S(1)}, f32[157,8,128]{2,1,0:T(8,128)S(1)}, u32[]{:S(2)}, u32[]{:S(2)}) collective-permute-start(f32[157,8,128]{2,1,0:T(8,128)S(1)} %get-tuple-element.26), channel_id=1, source_target_pairs={{16,32},{32,16},{48,64},{64,48},{80,96},{96,80},{112,128},{128,112... | collective-permute-start | bytes 1929224 | tf_op jit(solution)/shard_map/ppermute | solution.py:514
  19.7 0.1 shard_map.76
  19.7 1.9 %collective-permute-start.2 = (f32[156,8,128]{2,1,0:T(8,128)S(1)}, f32[156,8,128]{2,1,0:T(8,128)S(1)}, u32[]{:S(2)}, u32[]{:S(2)}) collective-permute-start(f32[156,8,128]{2,1,0:T(8,128)S(1)} %shard_map.76), channel_id=1, source_target_pairs={{0,16},{16,0},{32,48},{48,32},{64,80},{80,64},{96,112},{112,96},{1... | collective-permute-start | bytes 1916936 | tf_op jit(solution)/shard_map/ppermute | solution.py:523
  21.7 0.0 copy-done.2
  21.7 3.8 %shard_map.77 = (f32[600,8,128]{2,1,0:T(8,128)S(1)}, f32[16,8,128]{2,1,0:T(8,128)S(1)}) custom-call(f32[4800,128]{1,0:T(8,128)S(1)} %bitcast.34, f32[25]{0:T(128)S(1)} %copy-done.2, f32[8,128]{1,0:T(8,128)S(1)} %bitcast.37, f32[7,8,128]{2,1,0:T(8,128)S(1)} %get-tuple-element.18.joined), custom_call_target="tpu_custom_call" | custom-call | bytes 18000000 | tf_op jit(solution)/shard_map/pallas_call | solution.py:515
  25.5 0.0 copy-done.3
  25.5 0.0 copy-done.4
  25.5 0.0 copy-done.5
  25.5 0.0 copy-done.6
  25.5 1.1 %shard_map.78 = (f32[600,8,128]{2,1,0:T(8,128)S(1)}, f32[600,8,128]{2,1,0:T(8,128)S(1)}) custom-call(f32[25]{0:T(128)S(1)} %copy-done.6, f32[8,128]{1,0:T(8,128)S(1)} %bitcast.38, f32[8,128]{1,0:T(8,128)S(1)} %bitcast.39, s32[8,128]{1,0:T(8,128)S(1)} %bitcast.40, f32[600,8,128]{2,1,0:T(8,128)S(1)} %get-tuple-element.20.e_in), custom_call_target="tpu_custom_call" | custom-call | bytes 3600000 | tf_op jit(solution)/shard_map/pallas_call | solution.py:525
  26.6 0.0 collective-permute-done.2.a_in
  26.6 0.9 %shard_map.79 = (f32[200,8,128]{2,1,0:T(8,128)S(1)}, f32[16,8,128]{2,1,0:T(8,128)S(1)}) custom-call(f32[25]{0:T(128)S(1)} %copy-done.2, s32[1]{0:T(128)} %bitcast.odd_ref, f32[600,8,128]{2,1,0:T(8,128)S(1)} %get-tuple-element.22.f, f32[16,8,128]{2,1,0:T(8,128)S(1)} %get-tuple-element.23.mom, f32[156,8,128]{2,1,0:T(8,128)S(1)} %collective-permute-done.2.a_in, ...), custom_call_target="tpu_custom_call" | custom-call | tf_op jit(solution)/shard_map/pallas_call | solution.py:528
  27.5 0.2 collective-permute-done.3.z_in
  27.8 2.5 %shard_map.80 = f32[4800,128]{1,0:T(8,128)} custom-call(f32[25]{0:T(128)S(1)} %copy-done.2, s32[1]{0:T(128)} %bitcast.odd_ref, f32[600,8,128]{2,1,0:T(8,128)S(1)} %get-tuple-element.21.pf, f32[600,8,128]{2,1,0:T(8,128)S(1)} %get-tuple-element.22.f, f32[16,8,128]{2,1,0:T(8,128)S(1)} %get-tuple-element.24.mom, f32[200,8,128]{2,1,0:T(8,128)S(1)} %get-tuple-element.25.near, ...), custom_call_target="tpu_custom_call" | custom-call | bytes 10800000 | tf_op jit(solution)/shard_map/pallas_call | solution.py:529
Async XLA Ops:
  0.7 1.7 %copy-start = (f32[600,4,256]{2,1,0:T(4,128)S(1)}, f32[600,4,256]{2,1,0:T(4,128)}, u32[]{:S(2)}) copy-start(f32[600,4,256]{2,1,0:T(4,128)} %param.7) | copy-start | bytes 7372804
  2.4 6.1 %copy-start.1 = (f32[600,4,256]{2,1,0:T(4,128)S(1)}, f32[600,4,256]{2,1,0:T(4,128)}, u32[]{:S(2)}) copy-start(f32[600,4,256]{2,1,0:T(4,128)} %param.7) | copy-start | bytes 7372804
  3.0 18.7 %copy-start.2 = (f32[25]{0:T(128)S(1)}, f32[25]{0:T(128)}, u32[]{:S(2)}) copy-start(f32[25]{0:T(128)} %courant.5) | copy-start | bytes 304
  3.0 5.8 %collective-permute-start.1 = (f32[6,8,128]{2,1,0:T(8,128)S(1)}, f32[6,8,128]{2,1,0:T(8,128)S(1)}, u32[]{:S(2)}, u32[]{:S(2)}) collective-permute-start(f32[6,8,128]{2,1,0:T(8,128)S(1)} %shard_map.74), channel_id=1, source_target_pairs={{0,15},{1,2},{2,1},{3,4},{4,3},{5,6},{6,5},{7,8},{8,7},{9,10},{10,... | collective-permute-start | bytes 73736 | tf_op jit(solution)/shard_map/ppermute | solution.py:511
  5.1 7.9 %collective-permute-start = (f32[6,8,128]{2,1,0:T(8,128)S(1)}, f32[6,8,128]{2,1,0:T(8,128)S(1)}, u32[]{:S(2)}, u32[]{:S(2)}) collective-permute-start(f32[6,8,128]{2,1,0:T(8,128)S(1)} %shard_map.74), channel_id=1, source_target_pairs={{0,1},{1,0},{2,3},{3,2},{4,5},{5,4},{6,7},{7,6},{8,9},{9,8},{10,11... | collective-permute-start | bytes 73736 | tf_op jit(solution)/shard_map/ppermute | solution.py:511
  8.8 16.7 %copy-start.3 = (f32[4,256]{1,0:T(4,128)S(1)}, f32[4,256]{1,0:T(4,128)}, u32[]{:S(2)}) copy-start(f32[4,256]{1,0:T(4,128)} %param.9) | copy-start | bytes 12292
  8.8 16.7 %copy-start.4 = (f32[4,256]{1,0:T(4,128)S(1)}, f32[4,256]{1,0:T(4,128)}, u32[]{:S(2)}) copy-start(f32[4,256]{1,0:T(4,128)} %param.10) | copy-start | bytes 12292
  8.8 16.7 %copy-start.5 = (s32[4,256]{1,0:T(4,128)S(1)}, s32[4,256]{1,0:T(4,128)}, u32[]{:S(2)}) copy-start(s32[4,256]{1,0:T(4,128)} %param.12) | copy-start | bytes 12292
  8.8 16.7 %copy-start.6 = (f32[25]{0:T(128)S(1)}, f32[25]{0:T(128)}, u32[]{:S(2)}) copy-start(f32[25]{0:T(128)} %constant.29.clone.ratio_ref) | copy-start | bytes 304
  13.1 14.7 %collective-permute-start.3 = (f32[157,8,128]{2,1,0:T(8,128)S(1)}, f32[157,8,128]{2,1,0:T(8,128)S(1)}, u32[]{:S(2)}, u32[]{:S(2)}) collective-permute-start(f32[157,8,128]{2,1,0:T(8,128)S(1)} %get-tuple-element.26), channel_id=1, source_target_pairs={{16,32},{32,16},{48,64},{64,48},{80,96},{96,80},{112,128},{128,112... | collective-permute-start | bytes 1929224 | tf_op jit(solution)/shard_map/ppermute | solution.py:514
  19.7 6.9 %collective-permute-start.2 = (f32[156,8,128]{2,1,0:T(8,128)S(1)}, f32[156,8,128]{2,1,0:T(8,128)S(1)}, u32[]{:S(2)}, u32[]{:S(2)}) collective-permute-start(f32[156,8,128]{2,1,0:T(8,128)S(1)} %shard_map.76), channel_id=1, source_target_pairs={{0,16},{16,0},{32,48},{48,32},{64,80},{80,64},{96,112},{112,96},{1... | collective-permute-start | bytes 1916936 | tf_op jit(solution)/shard_map/ppermute | solution.py:523
